TPU v7x, 256 devices: a whole 4x4x8 slice. The times are simulated.
256 devices in a mesh: grp: 8 (over x, z_lo), shard: 32 (over z_hi, y, core).
Axes of the slice: x: 4, y: 4, z: 8 (z_hi: 4, z_lo: 2; z = z_hi * 2 + z_lo), core: 2. Of those that a mesh axis runs over, the one named last changes fastest.
Arguments:
- voltages: bfloat16 [16, 4194304], P('grp', 'shard'), may hold values from -6 to 6
- eq_gain: float32 [16, 4096], P('grp'), may hold values from 0.5 to 2
- delays: float32 [1024, 16], replicated, may hold values from -16 to 16
Outputs:
- beam_power: bfloat16 [32, 8, 4096, 1024], P(None, 'grp', 'shard')
All inputs are finite; a program needn't handle non-finite values.
Results may differ from a plain program's by a relative error of at most 0.0054.
Values may be sent and summed in bfloat16 or wider, within the bound.
No kernel may reach another device: no remote copies, remote signals or barrier semaphores. Data moves between devices by JAX's collectives and lax.ppermute only.
A program may use at most 256 MiB of HBM per device.

v0:
```python
import math

import jax
import jax.numpy as jnp
from jax import lax
from jax.sharding import PartitionSpec as P

CHANNELS = 4096
TAPS = 16
INTEG = 2


def shifted(value, axis, steps):
    count = lax.axis_size(axis)
    initial, last = (max(0, -steps), min(count, count - steps))
    return lax.ppermute(value, axis, [(source, source + steps) for source in range(initial, last)])


def make_window(tap_count, length):
    total = tap_count * length
    places = jnp.arange(total).astype(jnp.float32)
    centred = (places - (total - 1) / 2.0) / length
    taper = 0.5 - 0.5 * jnp.cos(2.0 * math.pi / total * (places + 0.5))
    shaped = jnp.sinc(centred) * taper
    shaped = shaped / jnp.sqrt(jnp.sum(shaped * shaped))
    return shaped.reshape(tap_count, length)


def four_step(filtered):
    row_count = filtered.shape[0]
    length = filtered.shape[1]
    inner_len = 64
    outer_len = length // inner_len
    folded = filtered.reshape(row_count, outer_len, inner_len)
    outer_idx = jnp.arange(outer_len, dtype=jnp.int32)
    inner_idx = jnp.arange(inner_len, dtype=jnp.int32)
    half_idx = jnp.arange(inner_len // 2, dtype=jnp.int32)
    first_phase = (
        2.0
        * math.pi
        / outer_len
        * (outer_idx[:, None] * outer_idx[None, :] % outer_len).astype(jnp.float32)
    )
    first_cos = jnp.cos(first_phase)
    first_sin = -jnp.sin(first_phase)
    middle = lax.Precision.HIGH
    section_real = jnp.einsum("rnm,nk->rmk", folded, first_cos, precision=middle)
    section_imag = jnp.einsum("rnm,nk->rmk", folded, first_sin, precision=middle)
    twist_phase = (
        2.0
        * math.pi
        / length
        * (inner_idx[:, None] * outer_idx[None, :] % length).astype(jnp.float32)
    )
    twist_cos = jnp.cos(twist_phase)[None]
    twist_sin = -jnp.sin(twist_phase)[None]
    turned_real = section_real * twist_cos - section_imag * twist_sin
    turned_imag = section_real * twist_sin + section_imag * twist_cos
    second_phase = (
        2.0
        * math.pi
        / inner_len
        * (inner_idx[:, None] * half_idx[None, :] % inner_len).astype(jnp.float32)
    )
    second_cos = jnp.cos(second_phase)
    second_sin = -jnp.sin(second_phase)
    out_real = jnp.einsum("rmk,mj->rjk", turned_real, second_cos, precision=middle) - jnp.einsum(
        "rmk,mj->rjk", turned_imag, second_sin, precision=middle
    )
    out_imag = jnp.einsum("rmk,mj->rjk", turned_real, second_sin, precision=middle) + jnp.einsum(
        "rmk,mj->rjk", turned_imag, second_cos, precision=middle
    )
    return (out_real.reshape(row_count, length // 2), out_imag.reshape(row_count, length // 2))


def per_device(voltages, eq_gain, delays):
    length = 2 * CHANNELS
    inputs_here = voltages.shape[0]
    frames = voltages.reshape(inputs_here, -1, length)
    frame_count = frames.shape[1]
    earlier = shifted(frames[:, frame_count - (TAPS - 1) :, :], "shard", 1)
    joined = jnp.concatenate([earlier, frames], axis=1)
    window = make_window(TAPS, length)
    filtered = jnp.zeros((inputs_here, frame_count, length), jnp.float32)
    for tap_index in range(TAPS):
        filtered = filtered + window[tap_index][None, None, :] * joined[
            :, tap_index : tap_index + frame_count, :
        ].astype(jnp.float32)
    real_flat, imag_flat = four_step(filtered.reshape(inputs_here * frame_count, length))
    gain_rows = eq_gain[:, None, :]
    real_part = (real_flat.reshape(inputs_here, frame_count, CHANNELS) * gain_rows).astype(
        jnp.bfloat16
    )
    imag_part = (imag_flat.reshape(inputs_here, frame_count, CHANNELS) * gain_rows).astype(
        jnp.bfloat16
    )
    stacked = jnp.stack([real_part, imag_part])
    groups = lax.axis_size("grp")
    per_group = frame_count // groups
    turned = lax.all_to_all(
        lax.all_to_all(stacked, "grp", split_axis=2, concat_axis=1, tiled=True),
        "shard",
        split_axis=3,
        concat_axis=2,
        tiled=True,
    )
    everyone = turned.shape[1]
    spectra_here = turned.shape[2]
    chan_here = turned.shape[3]
    chan_major = jnp.transpose(turned, (0, 3, 1, 2))
    real_spec = chan_major[0]
    imag_spec = chan_major[1]
    span = min(16, chan_here)
    shard_at = lax.axis_index("shard")
    results = []
    for block_index in range(chan_here // span):
        first_chan = block_index * span
        piece_real = real_spec[first_chan : first_chan + span]
        piece_imag = imag_spec[first_chan : first_chan + span]
        chan_index = shard_at * chan_here + first_chan + jnp.arange(span, dtype=jnp.int32)
        factor = 1.0 + chan_index.astype(jnp.float32) / CHANNELS
        phases = 2.0 * math.pi * (delays[None, :, :] * factor[:, None, None])
        w_real = jnp.cos(phases).astype(jnp.bfloat16)
        w_imag = (-jnp.sin(phases)).astype(jnp.bfloat16)
        beam_real = jnp.einsum(
            "kit,kbi->ktb", piece_real, w_real, preferred_element_type=jnp.float32
        ) - jnp.einsum("kit,kbi->ktb", piece_imag, w_imag, preferred_element_type=jnp.float32)
        beam_imag = jnp.einsum(
            "kit,kbi->ktb", piece_real, w_imag, preferred_element_type=jnp.float32
        ) + jnp.einsum("kit,kbi->ktb", piece_imag, w_real, preferred_element_type=jnp.float32)
        power = beam_real * beam_real + beam_imag * beam_imag
        beam_count = power.shape[2]
        power = power.reshape(span, spectra_here // INTEG, INTEG, beam_count).sum(axis=2)
        results.append(power)
    intensity = jnp.concatenate(results, axis=0)
    scaled = (intensity / everyone).astype(jnp.bfloat16)
    beam_count = scaled.shape[2]
    ordered = jnp.transpose(scaled, (1, 0, 2))
    return ordered.reshape(spectra_here // per_group, per_group // INTEG, chan_here, beam_count)


def solution(mesh):
    placed = (P("grp", "shard"), P("grp", None), P())
    return jax.shard_map(
        per_device,
        mesh=mesh,
        in_specs=placed,
        out_specs=P(None, "grp", "shard", None),
        check_vma=False,
    )
```

profile of v0, /device:TPU:1, one launch (start us, length us, event | category | flops | bytes accessed | tf_op | source)
XLA Modules:
  0.0 454.6 jit_solution(15984213326548184658)
XLA Ops:
  29.9 14.9 %all_to_all.36 = bf16[2,2,16,4096]{3,1,0,2:T(2,128)(2,1)S(1)} all-to-all(bf16[2,2,16,4096]{3,1,0,2:T(2,128)(2,1)S(1)} %copy.41), channel_id=1, replica_groups=mesh['grp'=8,'shard'=32] {'grp'}, dimensions={2} | all-to-all | bytes 1048576 | tf_op jit(solution)/shard_map/all_to_all | solution.py:101
  45.5 6.9 %copy.44 = bf16[2,16,2,4096]{1,2,0,3:T(2,128)(2,1)} copy(bf16[2,16,2,4096]{3,2,1,0:T(2,128)(2,1)S(1)} %bitcast.143) | data formatting | bytes 1048576 | tf_op jit(solution)/shard_map/all_to_all | solution.py:101
  52.4 12.9 %reshape.231 = bf16[32,2,4096]{2,1,0:T(2,128)(2,1)} reshape(bf16[4096,2,2,16]{3,2,1,0:T(2,128)(2,1)} %bitcast.106) | data formatting | bytes 1048576
  65.3 17.2 %all-to-all-start.1 = ((bf16[32,2,4096]{2,1,0:T(2,128)(2,1)}), bf16[32,2,4096]{2,1,0:T(2,128)(2,1)S(1)}, u32[]{:S(2)}, u32[]{:S(2)}) async-start(bf16[32,2,4096]{2,1,0:T(2,128)(2,1)} %reshape.231), calls=%async_computation.1 | async-start | bytes 1048576 | tf_op jit(solution)/shard_map/all_to_all | solution.py:100
  82.6 18.3 %all-to-all-done.1 = bf16[32,2,4096]{2,1,0:T(2,128)(2,1)S(1)} async-done(((bf16[32,2,4096]{2,1,0:T(2,128)(2,1)}), bf16[32,2,4096]{2,1,0:T(2,128)(2,1)S(1)}, u32[]{:S(2)}, u32[]{:S(2)}) %all-to-all-start.1) | async-done | bytes 524320 | tf_op jit(solution)/shard_map/all_to_all | solution.py:100
  105.0 8.8 %copy.53 = bf16[2,16,2,32,128]{4,1,2,3,0:T(8,128)(2,1)S(1)} copy(bf16[2,16,2,32,128]{1,2,0,4,3:T(2,128)(2,1)} %bitcast.107) | data formatting | bytes 1048576 | tf_op jit(solution)/shard_map/all_to_all | solution.py:100
  189.9 5.7 %fusion.21 = f32[16,64,1024]{2,1,0:T(8,128)} fusion(f32[16]{0:T(128)S(1)} %multiply_add_fusion.15, f32[1024,16]{0,1:T(8,128)S(1)} %copy-done, bf16[2,128,16,64]{3,2,1,0:T(8,128)(2,1)S(1)} %bitcast.123), kind=kOutput, calls=%fused_computation.93 | convolution fusion | flops 34603008 | bytes 4325888 | tf_op jit(solution)/shard_map/kit,kbi->ktb/dot_general | solution.py:128
  243.8 6.0 %reshape.218 = f32[16,32,2,1024]{3,2,1,0:T(2,128)} reshape(f32[16,64,1024]{2,1,0:T(8,128)} %multiply_add_fusion.7) | data formatting | bytes 8388608 | tf_op jit(solution)/shard_map/reshape | solution.py:133
  249.8 7.4 %reduce_sum.82 = f32[16,32,1024]{2,1,0:T(8,128)S(1)} reduce(f32[16,32,2,1024]{3,2,1,0:T(2,128)} %reshape.218, f32[]{:T(128)} %constant.102.clone.1), dimensions={2}, to_apply=%region_1.2 | reduce | flops 524288 | bytes 6291460 | tf_op jit(solution)/shard_map/reduce_sum | solution.py:133
  260.2 8.0 %multiply_add_fusion.6 = f32[16,64,1024]{2,1,0:T(8,128)} fusion(f32[16,64,1024]{2,1,0:T(8,128)S(1)} %copy-done.2, f32[16,64,1024]{2,1,0:T(8,128)} %fusion.4, f32[16,64,1024]{2,1,0:T(8,128)} %fusion.14, f32[16]{0:T(128)S(1)} %multiply_add_fusion.19, f32[1024,16]{0,1:T(8,128)S(1)} %copy-done, bf16[2,128,16,64]{3,2,1,0:T(8,128)(2,1)S(1)} %bitcast.133), kind=kOutput, calls=%fused_computation.8 | convolution fusion | flops 39583744 | bytes 16908800 | tf_op jit(solution)/shard_map/kit,kbi->ktb/dot_general | solution.py:130
  268.1 6.1 %reshape.219 = f32[16,32,2,1024]{3,2,1,0:T(2,128)} reshape(f32[16,64,1024]{2,1,0:T(8,128)} %multiply_add_fusion.6) | data formatting | bytes 8388608 | tf_op jit(solution)/shard_map/reshape | solution.py:133
  274.2 7.4 %reduce_sum.83 = f32[16,32,1024]{2,1,0:T(8,128)S(1)} reduce(f32[16,32,2,1024]{3,2,1,0:T(2,128)} %reshape.219, f32[]{:T(128)} %constant.102.clone.1), dimensions={2}, to_apply=%region_2.3 | reduce | flops 524288 | bytes 6291460 | tf_op jit(solution)/shard_map/reduce_sum | solution.py:133
  281.6 8.6 %multiply_add_fusion.5 = f32[16,64,1024]{2,1,0:T(8,128)} fusion(f32[16,64,1024]{2,1,0:T(8,128)} %fusion.15, f32[16,64,1024]{2,1,0:T(8,128)} %fusion.5, f32[16,64,1024]{2,1,0:T(8,128)} %fusion.16, f32[16]{0:T(128)S(1)} %multiply_add_fusion.18, f32[1024,16]{0,1:T(8,128)S(1)} %copy-done, bf16[2,128,16,64]{3,2,1,0:T(8,128)(2,1)S(1)} %bitcast.134), kind=kOutput, calls=%fused_computation.7 | convolution fusion | flops 39583744 | bytes 16908800 | tf_op jit(solution)/shard_map/kit,kbi->ktb/dot_general | solution.py:130
  290.2 6.3 %reshape.220 = f32[16,32,2,1024]{3,2,1,0:T(2,128)} reshape(f32[16,64,1024]{2,1,0:T(8,128)} %multiply_add_fusion.5) | data formatting | bytes 8388608 | tf_op jit(solution)/shard_map/reshape | solution.py:133
  296.5 8.7 %reduce_sum.84 = f32[16,32,1024]{2,1,0:T(8,128)} reduce(f32[16,32,2,1024]{3,2,1,0:T(2,128)} %reshape.220, f32[]{:T(128)} %constant.102.clone.1), dimensions={2}, to_apply=%region_3.4 | reduce | flops 524288 | bytes 6291460 | tf_op jit(solution)/shard_map/reduce_sum | solution.py:133
  305.2 8.6 %multiply_add_fusion.4 = f32[16,64,1024]{2,1,0:T(8,128)} fusion(f32[16,64,1024]{2,1,0:T(8,128)} %fusion.17, f32[16,64,1024]{2,1,0:T(8,128)} %fusion.6, f32[16,64,1024]{2,1,0:T(8,128)} %fusion.18, f32[16]{0:T(128)S(1)} %multiply_add_fusion.17, f32[1024,16]{0,1:T(8,128)S(1)} %copy-done, bf16[2,128,16,64]{3,2,1,0:T(8,128)(2,1)S(1)} %bitcast.135), kind=kOutput, calls=%fused_computation.6 | convolution fusion | flops 39583744 | bytes 16908800 | tf_op jit(solution)/shard_map/kit,kbi->ktb/dot_general | solution.py:130
  313.8 6.0 %reshape.221 = f32[16,32,2,1024]{3,2,1,0:T(2,128)} reshape(f32[16,64,1024]{2,1,0:T(8,128)} %multiply_add_fusion.4) | data formatting | bytes 8388608 | tf_op jit(solution)/shard_map/reshape | solution.py:133
  319.7 8.7 %reduce_sum.85 = f32[16,32,1024]{2,1,0:T(8,128)} reduce(f32[16,32,2,1024]{3,2,1,0:T(2,128)} %reshape.221, f32[]{:T(128)} %constant.102.clone.1), dimensions={2}, to_apply=%region_4.5 | reduce | flops 524288 | bytes 6291460 | tf_op jit(solution)/shard_map/reduce_sum | solution.py:133
  328.5 8.6 %multiply_add_fusion.3 = f32[16,64,1024]{2,1,0:T(8,128)} fusion(f32[16,64,1024]{2,1,0:T(8,128)} %fusion.19, f32[16,64,1024]{2,1,0:T(8,128)} %fusion.7, f32[16,64,1024]{2,1,0:T(8,128)} %fusion.20, f32[16]{0:T(128)S(1)} %multiply_add_fusion.16, f32[1024,16]{0,1:T(8,128)S(1)} %copy-done, bf16[2,128,16,64]{3,2,1,0:T(8,128)(2,1)S(1)} %bitcast.136), kind=kOutput, calls=%fused_computation.5 | convolution fusion | flops 39583744 | bytes 16908800 | tf_op jit(solution)/shard_map/kit,kbi->ktb/dot_general | solution.py:130
  337.1 6.0 %reshape.222 = f32[16,32,2,1024]{3,2,1,0:T(2,128)} reshape(f32[16,64,1024]{2,1,0:T(8,128)} %multiply_add_fusion.3) | data formatting | bytes 8388608 | tf_op jit(solution)/shard_map/reshape | solution.py:133
  343.1 8.7 %reduce_sum.86 = f32[16,32,1024]{2,1,0:T(8,128)} reduce(f32[16,32,2,1024]{3,2,1,0:T(2,128)} %reshape.222, f32[]{:T(128)} %constant.102.clone.1), dimensions={2}, to_apply=%region_5.6 | reduce | flops 524288 | bytes 6291460 | tf_op jit(solution)/shard_map/reduce_sum | solution.py:133
  351.8 8.6 %multiply_add_fusion.2 = f32[16,64,1024]{2,1,0:T(8,128)} fusion(f32[16,64,1024]{2,1,0:T(8,128)} %fusion.21, f32[16,64,1024]{2,1,0:T(8,128)} %fusion.8, f32[16,64,1024]{2,1,0:T(8,128)} %fusion.22, f32[16]{0:T(128)S(1)} %multiply_add_fusion.15, f32[1024,16]{0,1:T(8,128)S(1)} %copy-done, bf16[2,128,16,64]{3,2,1,0:T(8,128)(2,1)S(1)} %bitcast.137), kind=kOutput, calls=%fused_computation.4 | convolution fusion | flops 39583744 | bytes 16908800 | tf_op jit(solution)/shard_map/kit,kbi->ktb/dot_general | solution.py:130
  360.4 6.0 %reshape.223 = f32[16,32,2,1024]{3,2,1,0:T(2,128)} reshape(f32[16,64,1024]{2,1,0:T(8,128)} %multiply_add_fusion.2) | data formatting | bytes 8388608 | tf_op jit(solution)/shard_map/reshape | solution.py:133
  366.4 8.8 %reduce_sum.87 = f32[16,32,1024]{2,1,0:T(8,128)} reduce(f32[16,32,2,1024]{3,2,1,0:T(2,128)} %reshape.223, f32[]{:T(128)} %constant.102.clone.1), dimensions={2}, to_apply=%region_6.7 | reduce | flops 524288 | bytes 6291460 | tf_op jit(solution)/shard_map/reduce_sum | solution.py:133
  375.2 8.6 %multiply_add_fusion.1 = f32[16,64,1024]{2,1,0:T(8,128)} fusion(f32[16,64,1024]{2,1,0:T(8,128)} %fusion.23, f32[16,64,1024]{2,1,0:T(8,128)} %fusion.9, f32[16,64,1024]{2,1,0:T(8,128)} %fusion.24, f32[16]{0:T(128)S(1)} %multiply_add_fusion.14, f32[1024,16]{0,1:T(8,128)S(1)} %copy-done, bf16[2,128,16,64]{3,2,1,0:T(8,128)(2,1)S(1)} %bitcast.138), kind=kOutput, calls=%fused_computation.3 | convolution fusion | flops 39583744 | bytes 16908800 | tf_op jit(solution)/shard_map/kit,kbi->ktb/dot_general | solution.py:130
  383.7 6.3 %reshape.224 = f32[16,32,2,1024]{3,2,1,0:T(2,128)} reshape(f32[16,64,1024]{2,1,0:T(8,128)} %multiply_add_fusion.1) | data formatting | bytes 8388608 | tf_op jit(solution)/shard_map/reshape | solution.py:133
  390.0 8.7 %reduce_sum.88 = f32[16,32,1024]{2,1,0:T(8,128)} reduce(f32[16,32,2,1024]{3,2,1,0:T(2,128)} %reshape.224, f32[]{:T(128)} %constant.102.clone.1), dimensions={2}, to_apply=%region_7.8 | reduce | flops 524288 | bytes 6291460 | tf_op jit(solution)/shard_map/reduce_sum | solution.py:133
  398.8 8.6 %multiply_add_fusion = f32[16,64,1024]{2,1,0:T(8,128)} fusion(f32[16,64,1024]{2,1,0:T(8,128)} %fusion.25, f32[16,64,1024]{2,1,0:T(8,128)} %fusion.10, f32[16,64,1024]{2,1,0:T(8,128)} %fusion.26, f32[16]{0:T(128)S(1)} %multiply_add_fusion.13, f32[1024,16]{0,1:T(8,128)S(1)} %copy-done, bf16[2,128,16,64]{3,2,1,0:T(8,128)(2,1)S(1)} %bitcast.139), kind=kOutput, calls=%fused_computation.2 | convolution fusion | flops 39583744 | bytes 16908800 | tf_op jit(solution)/shard_map/kit,kbi->ktb/dot_general | solution.py:130
  407.4 6.0 %reshape.225 = f32[16,32,2,1024]{3,2,1,0:T(2,128)} reshape(f32[16,64,1024]{2,1,0:T(8,128)} %multiply_add_fusion) | data formatting | bytes 8388608 | tf_op jit(solution)/shard_map/reshape | solution.py:133
  413.3 8.7 %reduce_sum.89 = f32[16,32,1024]{2,1,0:T(8,128)} reduce(f32[16,32,2,1024]{3,2,1,0:T(2,128)} %reshape.225, f32[]{:T(128)} %constant.102.clone.1), dimensions={2}, to_apply=%region_8.9 | reduce | flops 524288 | bytes 6291460 | tf_op jit(solution)/shard_map/reduce_sum | solution.py:133
  433.3 9.6 %fusion = bf16[32,1,128,1024]{3,0,2,1:T(8,128)(2,1)} fusion(f32[128,32,1024]{2,1,0:T(8,128)} %constant_dynamic-update-slice_fusion), kind=kLoop, calls=%fused_computation.1 | loop fusion | flops 8388608 | bytes 25165824 | tf_op jit(solution)/shard_map/reshape | solution.py:139
  442.9 11.5 %copy.48 = bf16[32,1,128,1024]{3,2,1,0:T(8,128)(2,1)} copy(bf16[32,1,128,1024]{3,0,2,1:T(8,128)(2,1)} %fusion) | data formatting | bytes 16777216 | tf_op jit(solution)/shard_map/reshape | solution.py:139
  (84 shorter events, 172.3 us)
Async XLA Ops:
  1.5 11.0 %collective-permute-start = (bf16[2,15,8192]{2,1,0:T(8,128)(2,1)S(1)}, bf16[2,15,8192]{2,1,0:T(8,128)(2,1)S(1)}, u32[]{:S(2)}, u32[]{:S(2)}) collective-permute-start(bf16[2,15,8192]{2,1,0:T(8,128)(2,1)S(1)} %slice.291), channel_id=1, source_target_pairs={{0,1},{1,2},{2,3},{3,4},{4,5},{5,6},{6,7},{7,8},{8,9},{9,10},{10,1... | collective-permute-start | bytes 1474568 | tf_op jit(solution)/shard_map/ppermute | solution.py:16
  18.4 1.3 copy-start.1
  26.9 2.3 copy-start.9
  65.3 35.6 %all-to-all-start.1 = ((bf16[32,2,4096]{2,1,0:T(2,128)(2,1)}), bf16[32,2,4096]{2,1,0:T(2,128)(2,1)S(1)}, u32[]{:S(2)}, u32[]{:S(2)}) async-start(bf16[32,2,4096]{2,1,0:T(2,128)(2,1)} %reshape.231), calls=%async_computation.1 | async-start | bytes 1048576 | tf_op jit(solution)/shard_map/all_to_all | solution.py:100
  104.9 9.9 %copy-start = (f32[1024,16]{0,1:T(8,128)S(1)}, f32[1024,16]{0,1:T(8,128)}, u32[]{:S(2)}) copy-start(f32[1024,16]{0,1:T(8,128)} %param.5) | copy-start | bytes 196612
  257.2 2.9 copy-start.2
  422.0 2.3 copy-start.3
  422.0 3.8 copy-start.4
  424.4 3.0 copy-start.5
  425.9 3.0 copy-start.6
  427.3 3.0 copy-start.7
  428.9 2.9 copy-start.8
where the time goes:
time: 462 us; the launch traced here: 455 us
  matrix products  198 us (43%)
  local copies, waits for them, and re-layouts  114 us (25%)
  other arithmetic  86.4 us (19%)
  starting transfers between devices  21.8 us (5%)
  waiting for transfers between devices  18.3 us (4%)
  blocking collectives  14.9 us (3%)
    reduce_sum x8, other arithmetic, per_device(): power.reshape(span, spectra_here // INTEG, INTEG, beam_count).sum(axis=2)  67.1 us
    dot_general x8, matrix products, per_device(): jnp.einsum('kit,kbi->ktb', piece_imag, w_real, preferred_element_type=jnp...  65.1 us
    reshape x8, local copies, waits for them, and re-layouts, per_device(): power.reshape(span, spectra_here // INTEG, INTEG, beam_count).sum(axis=2)  48.6 us
    dot_general x8, matrix products, per_device(): jnp.einsum('kit,kbi->ktb', piece_real, w_imag, preferred_element_type=jnp...  41.8 us
    dot_general x8, matrix products, per_device(): jnp.einsum('kit,kbi->ktb', piece_imag, w_imag, preferred_element_type=jnp...  41.2 us
    dot_general x8, matrix products, per_device(): jnp.einsum('kit,kbi->ktb', piece_real, w_real, preferred_element_type=jnp...  40.4 us
    unnamed x30, local copies, waits for them, and re-layouts  32.3 us
    all_to_all x1, waiting for transfers between devices, per_device(): lax.all_to_all(lax.all_to_all(stacked, 'grp', split_axis=2, concat_axis=1...  18.3 us
  transfers between devices with their start and end apart: 2, of which 1 were waited for; matrix products, arithmetic and copies ran while one was open for 1% of the time, Pallas kernels for 0%

commit v1 on v0

v1 whole, which is shorter than its diff:
```python
import math

import jax
import jax.numpy as jnp
import numpy as np
from jax import lax
from jax.experimental import pallas as pl
from jax.experimental.pallas import tpu as pltpu
from jax.sharding import PartitionSpec as P

CHANNELS = 4096
TAPS = 16
INPUTS = 16
LENGTH = 2 * CHANNELS
INNER = 64
LANES = 128
F32 = jnp.float32
BF16 = jnp.bfloat16


def shifted(value, axis, steps):
    count = lax.axis_size(axis)
    initial, last = (max(0, -steps), min(count, count - steps))
    return lax.ppermute(value, axis, [(source, source + steps) for source in range(initial, last)])


def split(values):
    high = values.astype(np.float32).astype(BF16)
    low = (values - high.astype(np.float64)).astype(np.float32).astype(BF16)
    return high, low


def window_table():
    total = TAPS * LENGTH
    places = np.arange(total, dtype=np.float64)
    centred = (places - (total - 1) / 2.0) / LENGTH
    taper = 0.5 - 0.5 * np.cos(2.0 * math.pi / total * (places + 0.5))
    shaped = np.sinc(centred) * taper
    shaped = shaped / np.sqrt(np.sum(shaped * shaped))
    return shaped.reshape(TAPS, INNER, LANES).astype(np.float32)


def first_table():
    idx = np.arange(INNER)
    phase = 2.0 * math.pi / INNER * (np.outer(idx, idx) % INNER)
    high, low = split(np.concatenate([np.cos(phase), -np.sin(phase)], axis=0))
    return np.concatenate([high, high, low], axis=1)


def twist_table():
    phase = 2.0 * math.pi / LENGTH * np.outer(np.arange(INNER), np.arange(LANES))
    return np.stack([np.cos(phase), -np.sin(phase)]).astype(np.float32)


def second_table():
    k1 = 2 * np.arange(32)[None, :] + np.arange(2)[:, None]
    phase = 2.0 * math.pi / LANES * (np.arange(LANES)[:, None, None] * k1[None] % LANES)
    cos, sin = np.cos(phase), np.sin(phase)
    from_real = np.stack([cos, -sin], axis=2).reshape(LANES, LANES)
    from_imag = np.stack([sin, cos], axis=2).reshape(LANES, LANES)
    return np.stack(split(np.concatenate([from_real, from_imag], axis=0)))


def dot(left, right):
    return jnp.dot(left, right, preferred_element_type=F32)


def parts_of(value):
    high = value.astype(BF16)
    return high, (value - high.astype(F32)).astype(BF16)


def front_kernel(own, halo, win, first, twist, second, gain, out, wide, flt, inter):
    for i in range(2):
        wide[i, 0:15] = halo[i].astype(F32)
        wide[i, 15:31] = own[i].astype(F32)

    def filter_step(step, carry):
        i = step // 8
        rows = pl.ds(pl.multiple_of((step % 8) * 8, 8), 8)
        taps = [win[p, rows, :] for p in range(TAPS)]
        xs = [wide[i, t, rows, :] for t in range(31)]
        for t in range(16):
            even = taps[0] * xs[t]
            odd = taps[1] * xs[t + 1]
            for p in range(2, TAPS, 2):
                even = even + taps[p] * xs[t + p]
                odd = odd + taps[p + 1] * xs[t + p + 1]
            flt[i, t, rows, :] = even + odd
        return carry

    lax.fori_loop(0, 16, filter_step, 0)

    low_lanes = lax.broadcasted_iota(jnp.int32, (64, LANES), 1) < 64

    def group_step(g, carry):
        columns = []
        for i in range(2):
            for j in range(2):
                high, low = parts_of(flt[i, 2 * g + j])
                columns.append(jnp.concatenate([high, low, high], axis=0))
        stage = dot(first[...], jnp.concatenate(columns, axis=1))
        t_re, t_im = twist[0], twist[1]
        turned = []
        for row in range(4):
            re = stage[:64, row * 128 : row * 128 + 128]
            im = stage[64:, row * 128 : row * 128 + 128]
            turned.append(
                jnp.concatenate([re * t_re - im * t_im, re * t_im + im * t_re], axis=1)
            )
        high, low = parts_of(jnp.concatenate(turned, axis=0))
        spec = dot(high, second[0]) + dot(low, second[0]) + dot(high, second[1])
        for i in range(2):
            flipped = spec[i * 128 : i * 128 + 128].T
            even, odd = flipped[:64], flipped[64:]
            rows = (
                jnp.where(low_lanes, even, pltpu.roll(odd, 64, 1)),
                jnp.where(low_lanes, pltpu.roll(even, 64, 1), odd),
            )
            for j in range(2):
                for part in range(2):
                    place = part * 4 + i * 2 + j
                    inter[pl.ds(place, 32, stride=8), :] = (
                        rows[j][part * 32 : part * 32 + 32] * gain[i]
                    )
        out[g] = inter[0:256].astype(BF16)
        return carry

    lax.fori_loop(0, 8, group_step, 0)


def front(own, halo, gain):
    args = (
        own,
        halo,
        jnp.asarray(window_table()),
        jnp.asarray(first_table()),
        jnp.asarray(twist_table()),
        jnp.asarray(second_table()),
        gain,
    )
    return pl.pallas_call(
        front_kernel,
        out_shape=jax.ShapeDtypeStruct((8, 256, LANES), BF16),
        scratch_shapes=[
            pltpu.VMEM((2, 31, INNER, LANES), F32),
            pltpu.VMEM((2, 16, INNER, LANES), F32),
            pltpu.VMEM((264, LANES), F32),
        ],
        compiler_params=pltpu.CompilerParams(vmem_limit_bytes=58 << 20),
        cost_estimate=pl.CostEstimate(flops=400_000_000, bytes_accessed=3_000_000, transcendentals=0),
        name="front",
    )(*args)


def weight_kernel(base, turn, out, carry):
    @pl.when(pl.program_id(0) == 0)
    def _():
        carry[...] = base[...]

    for block in range(4):
        cols = pl.ds(block * 256, 256)
        re, im = carry[0, :, cols], carry[1, :, cols]
        t_re, t_im = turn[0, :, cols], turn[1, :, cols]
        for c in range(8):
            out[0, c * 32 : c * 32 + 16, cols] = re.astype(BF16)
            out[0, c * 32 + 16 : c * 32 + 32, cols] = im.astype(BF16)
            re, im = re * t_re - im * t_im, re * t_im + im * t_re
        carry[0, :, cols] = re
        carry[1, :, cols] = im


def weights(delays, first_chan, chan_here):
    beams = delays.shape[0]
    rows = jnp.transpose(delays.reshape(beams, 8, 2), (2, 1, 0)).reshape(INPUTS, beams)
    factor = 1.0 + first_chan.astype(F32) / CHANNELS
    phase = 2.0 * math.pi * (rows * factor)
    base = jnp.stack([jnp.cos(phase), -jnp.sin(phase)])
    step = (2.0 * math.pi / CHANNELS) * rows
    turn = jnp.stack([jnp.cos(step), -jnp.sin(step)])
    groups = chan_here // 8
    whole = pl.BlockSpec((2, INPUTS, beams), lambda k: (0, 0, 0))
    return pl.pallas_call(
        weight_kernel,
        grid=(groups,),
        in_specs=[whole, whole],
        out_specs=pl.BlockSpec((1, 256, beams), lambda k: (k, 0, 0)),
        out_shape=jax.ShapeDtypeStruct((groups, 256, beams), BF16),
        scratch_shapes=[pltpu.VMEM((2, INPUTS, beams), F32)],
        compiler_params=pltpu.CompilerParams(vmem_limit_bytes=50 << 20),
        cost_estimate=pl.CostEstimate(flops=20_000_000, bytes_accessed=9_000_000, transcendentals=0),
        name="weights",
    )(base, turn)


def beam_kernel(spec, w, out, wide, flat, lhs):
    step = pl.program_id(0)

    @pl.when(step == 0)
    def _():
        wide[0:2048] = spec[...].astype(F32)

        def turn(q, carry):
            j, four = q // 8, q % 8
            straight, crossed = [], []
            for p in range(4):
                row = (four * 4 + p) * 8 + j
                got = [wide[pl.ds(row + 2 * r, 8, stride=256), :] for r in range(4)]
                straight += [got[0], got[1], -got[2], -got[3]]
                crossed += [got[2], got[3], got[0], got[1]]
            flat[0, q] = jnp.concatenate(straight, axis=0).T
            flat[1, q] = jnp.concatenate(crossed, axis=0).T
            return carry

        lax.fori_loop(0, 16, turn, 0)

    lane = lax.broadcasted_iota(jnp.int32, (8, LANES), 1) // 32
    chan = lax.broadcasted_iota(jnp.int32, (8, LANES), 0)
    bit0, bit1 = chan % 2 == 1, chan // 2 % 2 == 1
    masks = [jnp.where(chan == lane + 4 * half, 1.0, 0.0).astype(F32) for half in range(2)]
    for group in range(2):
        rows = pl.ds(pl.multiple_of(step * 16 + group * 8, 8), 8)
        for v in range(2):
            for q in range(16):
                spread = flat[v, q, rows, :]
                spread = jnp.where(bit0, pltpu.roll(spread, 32, 1), spread)
                spread = jnp.where(bit1, pltpu.roll(spread, 64, 1), spread)
                each = [spread] + [pltpu.roll(spread, 128 - 32 * p, 1) for p in range(1, 4)]
                at = (v * 16 + q) * 32
                for half in range(2):
                    block = jnp.concatenate([e * masks[half] for e in each], axis=0)
                    lhs[group, at : at + 32, half * 128 : half * 128 + 128] = block.astype(BF16)
    for n in range(4):
        cols = pl.ds(n * 256, 256)
        powers = []
        for group in range(2):
            amp = dot(lhs[group], w[group, :, cols])
            amp = amp * amp
            total = (amp[0:256] + amp[256:512]) + (amp[512:768] + amp[768:1024])
            powers.append(total.reshape(32, 8, 256))
        both = jnp.concatenate(powers, axis=1) * (1.0 / INPUTS)
        out[:, 0, :, cols] = both.astype(BF16)


def beams_of(spec, w, chan_here):
    count = w.shape[2]
    return pl.pallas_call(
        beam_kernel,
        grid=(chan_here // 16,),
        in_specs=[
            pl.BlockSpec((2048, LANES), lambda k: (0, 0)),
            pl.BlockSpec((2, 256, count), lambda k: (k, 0, 0)),
        ],
        out_specs=pl.BlockSpec((32, 1, 16, count), lambda k: (0, 0, k, 0)),
        out_shape=jax.ShapeDtypeStruct((32, 1, chan_here, count), BF16),
        scratch_shapes=[
            pltpu.VMEM((2304, LANES), F32),
            pltpu.VMEM((2, 16, LANES, LANES), F32),
            pltpu.VMEM((2, 1024, 256), BF16),
        ],
        compiler_params=pltpu.CompilerParams(vmem_limit_bytes=58 << 20),
        cost_estimate=pl.CostEstimate(flops=9_000_000_000, bytes_accessed=17_000_000, transcendentals=0),
        name="beams",
    )(spec, w)


def per_device(voltages, eq_gain, delays):
    frames = voltages.reshape(2, 16, INNER, LANES)
    halo = shifted(frames[:, 1:], "shard", 1)
    chan_here = CHANNELS // lax.axis_size("shard")
    messages = front(frames, halo, eq_gain.reshape(2, 32, LANES))
    got = lax.all_to_all(
        messages.reshape(256, 8, LANES), ("grp", "shard"), split_axis=0, concat_axis=0, tiled=True
    )
    w = weights(delays, lax.axis_index("shard") * chan_here, chan_here)
    return beams_of(got.reshape(2048, LANES), w, chan_here)


def solution(mesh):
    placed = (P("grp", "shard"), P("grp", None), P())
    return jax.shard_map(
        per_device,
        mesh=mesh,
        in_specs=placed,
        out_specs=P(None, "grp", "shard", None),
        check_vma=False,
    )
```

time: 462 us -> 83.2 us (0.18); the launches traced: 455 us -> 82.8 us
  matrix products: 198 us -> 0 us
  local copies, waits for them, and re-layouts: 114 us -> 4.38 us
  other arithmetic: 86.4 us -> 1.34 us
  Pallas kernels: 0 us -> 34.1 us
  blocking collectives: 14.9 us -> 0 us
  starting transfers between devices: 21.8 us -> 26.9 us
    dot_general x38 -> x0, matrix products: 198 us -> none  [the longest x8 65.1 us: per_device(): jnp.einsum('kit,kbi->ktb', piece_imag, w_real, preferred_element_type=jnp...]
    reduce_sum x9 -> x0, other arithmetic: 70.2 us -> none  [the longest x8 67.1 us: per_device(): power.reshape(span, spectra_here // INTEG, INTEG, beam_count).sum(axis=2)]
    reshape x9 -> x0, local copies, waits for them, and re-layouts: 60.1 us -> none  [the longest x8 48.6 us: per_device(): power.reshape(span, spectra_here // INTEG, INTEG, beam_count).sum(axis=2)]
    pallas_call x0 -> x3, Pallas kernels: none -> 34.1 us  [the longest x1 17.9 us: beams_of(): pl.pallas_call(beam_kernel, grid=(chan_here // 16,), in_specs=[pl.BlockSp...]
    unnamed x30 -> x8, local copies, waits for them, and re-layouts: 32.3 us -> 4.09 us
    all_to_all x4 -> x0, local copies, waits for them, and re-layouts: 17.4 us -> none  [the longest x2 9.85 us: per_device(): lax.all_to_all(lax.all_to_all(stacked, 'grp', split_axis=2, concat_axis=1...]
    all_to_all x1 -> x0, blocking collectives: 14.9 us -> none  [per_device(): lax.all_to_all(stacked, 'grp', split_axis=2, concat_axis=1, tiled=True)]
    reshape x1 -> x0, other arithmetic: 9.63 us -> none  [per_device(): ordered.reshape(spectra_here // per_group, per_group // INTEG, chan_here,...]
  transfers between devices with their start and end apart: 2 -> 2, of which waited for: 1 -> 2; matrix products, arithmetic and copies ran while one was open for 1% -> 4% of each run, Pallas kernels for 0% -> 9%
where the time goes in v1:
time: 83.2 us; the launch traced here: 82.8 us
  Pallas kernels  34.1 us (41%)
  starting transfers between devices  26.9 us (32%)
  waiting for transfers between devices  16.1 us (19%)
  local copies, waits for them, and re-layouts  4.38 us (5%)
  other arithmetic  1.34 us (2%)
    all_to_all x1, starting transfers between devices, per_device(): lax.all_to_all(messages.reshape(256, 8, LANES), ('grp', 'shard'), split_a...  22.3 us
    pallas_call x1, Pallas kernels, beams_of(): pl.pallas_call(beam_kernel, grid=(chan_here // 16,), in_specs=[pl.BlockSp...  17.9 us
    all_to_all x1, waiting for transfers between devices, per_device(): lax.all_to_all(messages.reshape(256, 8, LANES), ('grp', 'shard'), split_a...  11.7 us
    pallas_call x1, Pallas kernels, front(): pl.pallas_call(front_kernel, out_shape=jax.ShapeDtypeStruct((8, 256, LANE...  8.54 us
    pallas_call x1, Pallas kernels, weights(): pl.pallas_call(weight_kernel, grid=(groups,), in_specs=[whole, whole], ou...  7.63 us
    ppermute x1, starting transfers between devices, shifted(): lax.ppermute(value, axis, [(source, source + steps) for source in range(i...  4.59 us
    ppermute x1, waiting for transfers between devices, shifted(): lax.ppermute(value, axis, [(source, source + steps) for source in range(i...  4.38 us
    unnamed x8, local copies, waits for them, and re-layouts  4.09 us
  transfers between devices with their start and end apart: 2, of which 2 were waited for; matrix products, arithmetic and copies ran while one was open for 4% of the time, Pallas kernels for 9%

profile of v1, /device:TPU:1, one launch (start us, length us, event | category | flops | bytes accessed | tf_op | source)
XLA Modules:
  0.0 82.8 jit_solution(9317540384056573092)
XLA Ops:
  0.0 1.1 %copy.12 = bf16[1,2,1024,128]{3,2,1,0:T(8,128)(2,1)S(1)} copy(bf16[1,2,1024,128]{3,1,2,0:T(2,128)(2,1)} %bitcast.36) | data formatting | bytes 1048576
  1.1 0.0 copy-start
  1.2 4.6 %collective-permute-start = (bf16[2,15,64,128]{3,2,1,0:T(8,128)(2,1)S(1)}, bf16[2,15,64,128]{3,2,1,0:T(8,128)(2,1)S(1)}, u32[]{:S(2)}, u32[]{:S(2)}) collective-permute-start(bf16[2,15,64,128]{3,2,1,0:T(8,128)(2,1)S(1)} %slice.4), channel_id=1, source_target_pairs={{0,1},{1,2},{2,3},{3,4},{4,5},{5,6},{6,7},{7,8},{8,9},{9,10},{10,1... | collective-permute-start | bytes 1474568 | tf_op jit(solution)/shard_map/ppermute | solution.py:24
  5.8 1.4 %copy.19 = f32[1,2,32,128]{3,2,1,0:T(8,128)} copy(f32[1,2,32,128]{3,1,2,0:T(2,128)} %bitcast.39) | data formatting | bytes 65536
  7.1 4.4 %collective-permute-done.halo = bf16[2,15,64,128]{3,2,1,0:T(8,128)(2,1)S(1)} collective-permute-done((bf16[2,15,64,128]{3,2,1,0:T(8,128)(2,1)S(1)}, bf16[2,15,64,128]{3,2,1,0:T(8,128)(2,1)S(1)}, u32[]{:S(2)}, u32[]{:S(2)}) %collective-permute-start) | collective-permute-done | bytes 491552 | tf_op jit(solution)/shard_map/ppermute | solution.py:24
  11.5 0.0 copy-start.2
  11.5 0.0 copy-done
  11.5 0.8 copy-done.2
  12.3 8.5 %front.1 = bf16[8,256,128]{2,1,0:T(8,128)(2,1)} custom-call(bf16[2,16,64,128]{3,2,1,0:T(8,128)(2,1)} %bitcast.34, bf16[2,15,64,128]{3,2,1,0:T(8,128)(2,1)} %copy-done.2, f32[16,64,128]{2,1,0:T(8,128)} %constant.23.clone.win, bf16[128,192]{1,0:T(8,128)(2,1)} %constant.24.clone.first, f32[2,64,128]{2,1,0:T(8,128)} %constant.25.clone.twist, ...), custom_call_target="tpu_custom_call" | custom-call | flops 400000000 | bytes 3000000 | tf_op jit(solution)/shard_map/front/pallas_call | solution.py:142
  20.8 22.3 %all-to-all-start = ((bf16[256,8,128]{2,1,0:T(8,128)(2,1)}), bf16[256,8,128]{2,1,0:T(8,128)(2,1)S(1)}, u32[]{:S(2)}, u32[]{:S(2)}) async-start(bf16[256,8,128]{2,1,0:T(8,128)(2,1)} %bitcast.35), calls=%async_computation | async-start | bytes 1048576 | tf_op jit(solution)/shard_map/all_to_all | solution.py:272
  43.1 1.3 %multiply_cosine_fusion = (f32[1024,16]{0,1:T(8,128)S(1)}, f32[1024,16]{0,1:T(8,128)S(1)}, f32[1024,16]{0,1:T(8,128)S(1)}, f32[1024,16]{0,1:T(8,128)S(1)}) fusion(f32[1024,16]{0,1:T(8,128)} %param.9, f32[]{:T(128)S(6)} %add_shard_map.3), kind=kLoop, calls=%fused_computation.9 | loop fusion | flops 81920 | bytes 327684 | tf_op jit(solution)/shard_map/cos | solution.py:180
  44.8 7.6 %weights.1.w = bf16[16,256,1024]{2,1,0:T(8,128)(2,1)} custom-call(f32[2,16,1024]{2,1,0:T(8,128)S(1)} %pad_maximum_fusion.base, f32[2,16,1024]{2,1,0:T(8,128)S(1)} %pad_maximum_fusion.1.turn), custom_call_target="tpu_custom_call" | custom-call | flops 20000000 | bytes 9000000 | tf_op jit(solution)/shard_map/weights/pallas_call | solution.py:183
  52.4 11.7 %all-to-all-done = bf16[256,8,128]{2,1,0:T(8,128)(2,1)S(1)} async-done(((bf16[256,8,128]{2,1,0:T(8,128)(2,1)}), bf16[256,8,128]{2,1,0:T(8,128)(2,1)S(1)}, u32[]{:S(2)}, u32[]{:S(2)}) %all-to-all-start) | async-done | bytes 524320 | tf_op jit(solution)/shard_map/all_to_all | solution.py:272
  64.1 0.0 copy-start.1
  64.1 0.8 %copy-done.1 = bf16[256,8,128]{2,1,0:T(8,128)(2,1)} copy-done((bf16[256,8,128]{2,1,0:T(8,128)(2,1)}, bf16[256,8,128]{2,1,0:T(8,128)(2,1)S(1)}, u32[]{:S(2)}) %copy-start.1) | copy-done | bytes 524312
  64.9 17.9 %beams.1 = bf16[32,1,128,1024]{3,2,1,0:T(8,128)(2,1)} custom-call(bf16[2048,128]{1,0:T(8,128)(2,1)} %bitcast.37, bf16[16,256,1024]{2,1,0:T(8,128)(2,1)} %weights.1.w), custom_call_target="tpu_custom_call" | custom-call | flops 8999999488 | bytes 17000000 | tf_op jit(solution)/shard_map/beams/pallas_call | solution.py:247
  (9 shorter events, 0.3 us)
Async XLA Ops:
  1.1 10.4 %copy-start = (bf16[1,2,1024,128]{3,2,1,0:T(8,128)(2,1)}, bf16[1,2,1024,128]{3,2,1,0:T(8,128)(2,1)S(1)}, u32[]{:S(2)}) copy-start(bf16[1,2,1024,128]{3,2,1,0:T(8,128)(2,1)S(1)} %copy.12) | copy-start | bytes 1572868
  1.2 10.4 %collective-permute-start = (bf16[2,15,64,128]{3,2,1,0:T(8,128)(2,1)S(1)}, bf16[2,15,64,128]{3,2,1,0:T(8,128)(2,1)S(1)}, u32[]{:S(2)}, u32[]{:S(2)}) collective-permute-start(bf16[2,15,64,128]{3,2,1,0:T(8,128)(2,1)S(1)} %slice.4), channel_id=1, source_target_pairs={{0,1},{1,2},{2,3},{3,4},{4,5},{5,6},{6,7},{7,8},{8,9},{9,10},{10,1... | collective-permute-start | bytes 1474568 | tf_op jit(solution)/shard_map/ppermute | solution.py:24
  11.5 0.8 copy-start.2
  20.8 43.2 %all-to-all-start = ((bf16[256,8,128]{2,1,0:T(8,128)(2,1)}), bf16[256,8,128]{2,1,0:T(8,128)(2,1)S(1)}, u32[]{:S(2)}, u32[]{:S(2)}) async-start(bf16[256,8,128]{2,1,0:T(8,128)(2,1)} %bitcast.35), calls=%async_computation | async-start | bytes 1048576 | tf_op jit(solution)/shard_map/all_to_all | solution.py:272
  64.1 0.8 %copy-start.1 = (bf16[256,8,128]{2,1,0:T(8,128)(2,1)}, bf16[256,8,128]{2,1,0:T(8,128)(2,1)S(1)}, u32[]{:S(2)}) copy-start(bf16[256,8,128]{2,1,0:T(8,128)(2,1)S(1)} %all-to-all-done) | copy-start | bytes 1572868

commit v2 on v1

v2 whole, which is shorter than its diff:
```python
import math

import jax
import jax.numpy as jnp
import numpy as np
from jax import lax
from jax.experimental import pallas as pl
from jax.experimental.pallas import tpu as pltpu
from jax.sharding import PartitionSpec as P

CHANNELS = 4096
TAPS = 16
INPUTS = 16
LENGTH = 2 * CHANNELS
INNER = 64
LANES = 128
F32 = jnp.float32
BF16 = jnp.bfloat16


def split(values):
    high = values.astype(np.float32).astype(BF16)
    low = (values - high.astype(np.float64)).astype(np.float32).astype(BF16)
    return high, low


def window_table():
    total = TAPS * LENGTH
    places = np.arange(total, dtype=np.float64)
    centred = (places - (total - 1) / 2.0) / LENGTH
    taper = 0.5 - 0.5 * np.cos(2.0 * math.pi / total * (places + 0.5))
    shaped = np.sinc(centred) * taper
    shaped = shaped / np.sqrt(np.sum(shaped * shaped))
    return shaped.reshape(TAPS, INNER, LANES).astype(np.float32)


def first_table():
    idx = np.arange(INNER)
    phase = 2.0 * math.pi / INNER * (np.outer(idx, idx) % INNER)
    high, low = split(np.concatenate([np.cos(phase), -np.sin(phase)], axis=0))
    return np.concatenate([high, high, low], axis=1)


def twist_table():
    phase = 2.0 * math.pi / LENGTH * np.outer(np.arange(INNER), np.arange(LANES))
    return np.stack([np.cos(phase), -np.sin(phase)]).astype(np.float32)


def second_table():
    k1 = 2 * np.arange(32)[None, :] + np.arange(2)[:, None]
    phase = 2.0 * math.pi / LANES * (np.arange(LANES)[:, None, None] * k1[None] % LANES)
    cos, sin = np.cos(phase), np.sin(phase)
    from_real = np.stack([cos, -sin], axis=2).reshape(LANES, LANES)
    from_imag = np.stack([sin, cos], axis=2).reshape(LANES, LANES)
    return np.stack(split(np.concatenate([from_real, from_imag], axis=0)))


def dot(left, right):
    return jnp.dot(left, right, preferred_element_type=F32)


def parts_of(value):
    high = value.astype(BF16)
    return high, (value - high.astype(F32)).astype(BF16)


def summed(terms):
    lanes = [terms[0], terms[1]] if len(terms) > 1 else [terms[0]]
    for at, term in enumerate(terms[2:]):
        lanes[at % 2] = lanes[at % 2] + term
    return lanes[0] + lanes[1] if len(lanes) > 1 else lanes[0]


def front_kernel(
    keep, before, own, after, win_far, first_far, twist_far, second_far, gain, out,
    wide, flt, inter, win, first, twist, second, arrived,
):
    tables = ((win_far, win), (first_far, first), (twist_far, twist), (second_far, second))
    copies = [
        pltpu.make_async_copy(far, near, arrived.at[at]) for at, (far, near) in enumerate(tables)
    ]
    for copy in copies:
        copy.start()
    for i in range(2):
        wide[i, 0:7] = before[i].astype(F32)
        wide[i, 7:23] = own[i].astype(F32)
        wide[i, 23:31] = after[i].astype(F32)
    keep_old = keep[0]
    for copy in copies:
        copy.wait()

    def filter_step(step, carry):
        i = step // 8
        rows = pl.ds(pl.multiple_of((step % 8) * 8, 8), 8)
        taps = [win[p, rows, :] for p in range(TAPS)]
        xs = [wide[i, t, rows, :] for t in range(31)]
        for t in range(16):
            terms = [taps[p] * xs[t + p] for p in range(TAPS)]
            cut = 23 - t
            if cut >= TAPS:
                total = summed(terms)
            else:
                total = summed(terms[:cut]) * keep_old + summed(terms[cut:])
            flt[i, t, rows, :] = total
        return carry

    lax.fori_loop(0, 16, filter_step, 0)

    low_lanes = lax.broadcasted_iota(jnp.int32, (64, LANES), 1) < 64

    def group_step(g, carry):
        columns = []
        for i in range(2):
            for j in range(2):
                high, low = parts_of(flt[i, 2 * g + j])
                columns.append(jnp.concatenate([high, low, high], axis=0))
        stage = dot(first[...], jnp.concatenate(columns, axis=1))
        t_re, t_im = twist[0], twist[1]
        turned = []
        for row in range(4):
            re = stage[:64, row * 128 : row * 128 + 128]
            im = stage[64:, row * 128 : row * 128 + 128]
            turned.append(
                jnp.concatenate([re * t_re - im * t_im, re * t_im + im * t_re], axis=1)
            )
        high, low = parts_of(jnp.concatenate(turned, axis=0))
        spec = dot(high, second[0]) + dot(low, second[0]) + dot(high, second[1])
        for i in range(2):
            flipped = spec[i * 128 : i * 128 + 128].T
            even, odd = flipped[:64], flipped[64:]
            rows = (
                jnp.where(low_lanes, even, pltpu.roll(odd, 64, 1)),
                jnp.where(low_lanes, pltpu.roll(even, 64, 1), odd),
            )
            for j in range(2):
                for part in range(2):
                    place = part * 4 + i * 2 + j
                    inter[g, pl.ds(place, 32, stride=8), :] = (
                        rows[j][part * 32 : part * 32 + 32] * gain[i]
                    )
        out[(g + 4) % 8] = inter[g, 0:256].astype(BF16)
        return carry

    for g in range(8):
        group_step(g, 0)


def far(table):
    return pltpu.with_memory_space_constraint(jnp.asarray(table), pltpu.HBM)


def front(keep, before, own, after, gain):
    args = (
        keep,
        before,
        own,
        after,
        far(window_table()),
        far(first_table()),
        far(twist_table()),
        far(second_table()),
        gain,
    )
    return pl.pallas_call(
        front_kernel,
        in_specs=[pl.BlockSpec(memory_space=pltpu.SMEM)]
        + [pl.BlockSpec(memory_space=pltpu.VMEM)] * 3
        + [pl.BlockSpec(memory_space=pltpu.HBM)] * 4
        + [pl.BlockSpec(memory_space=pltpu.VMEM)],
        out_shape=jax.ShapeDtypeStruct((8, 256, LANES), BF16),
        scratch_shapes=[
            pltpu.VMEM((2, 31, INNER, LANES), F32),
            pltpu.VMEM((2, 16, INNER, LANES), F32),
            pltpu.VMEM((8, 264, LANES), F32),
            pltpu.VMEM((TAPS, INNER, LANES), F32),
            pltpu.VMEM((128, 192), BF16),
            pltpu.VMEM((2, INNER, LANES), F32),
            pltpu.VMEM((2, 256, LANES), BF16),
            pltpu.SemaphoreType.DMA((4,)),
        ],
        compiler_params=pltpu.CompilerParams(vmem_limit_bytes=24 << 20),
        cost_estimate=pl.CostEstimate(flops=400_000_000, bytes_accessed=3_000_000, transcendentals=0),
        name="front",
    )(*args)


def weight_kernel(base, turn, out, carry):
    @pl.when(pl.program_id(0) == 0)
    def _():
        carry[...] = base[...]

    for block in range(4):
        cols = pl.ds(block * 256, 256)
        re, im = carry[0, :, cols], carry[1, :, cols]
        t_re, t_im = turn[0, :, cols], turn[1, :, cols]
        for c in range(16):
            half, at = c // 8, c % 8 * 32
            out[half, at : at + 16, cols] = re.astype(BF16)
            out[half, at + 16 : at + 32, cols] = im.astype(BF16)
            re, im = re * t_re - im * t_im, re * t_im + im * t_re
        carry[0, :, cols] = re
        carry[1, :, cols] = im


def angles(delays, first_chan):
    beams = delays.shape[0]
    rows = jnp.transpose(delays.reshape(beams, 8, 2), (2, 1, 0)).reshape(INPUTS, beams)
    factor = 1.0 + first_chan.astype(F32) / CHANNELS
    phase = 2.0 * math.pi * (rows * factor)
    base = jnp.stack([jnp.cos(phase), -jnp.sin(phase)])
    step = (2.0 * math.pi / CHANNELS) * rows
    turn = jnp.stack([jnp.cos(step), -jnp.sin(step)])
    return base, turn


def weights(base, turn, chan_here):
    beams = base.shape[2]
    groups = chan_here // 8
    whole = pl.BlockSpec((2, INPUTS, beams), lambda k: (0, 0, 0))
    return pl.pallas_call(
        weight_kernel,
        grid=(groups // 2,),
        in_specs=[whole, whole],
        out_specs=pl.BlockSpec((2, 256, beams), lambda k: (k, 0, 0)),
        out_shape=jax.ShapeDtypeStruct((groups, 256, beams), BF16),
        scratch_shapes=[pltpu.VMEM((2, INPUTS, beams), F32)],
        compiler_params=pltpu.CompilerParams(vmem_limit_bytes=54 << 20),
        cost_estimate=pl.CostEstimate(flops=20_000_000, bytes_accessed=9_000_000, transcendentals=0),
        name="weights",
    )(base, turn)


def beam_kernel(lag, spec, w, out, wide, flat, left, right):
    step = pl.program_id(0)
    lane = lax.broadcasted_iota(jnp.int32, (8, LANES), 1) // 32
    chan = lax.broadcasted_iota(jnp.int32, (8, LANES), 0)
    bit0, bit1 = chan % 2 == 1, chan // 2 % 2 == 1
    masks = [jnp.where(chan == lane + 4 * half, 1.0, 0.0).astype(F32) for half in range(2)]

    def spread_out(first_chan, lhs):
        rows = pl.ds(pl.multiple_of(first_chan, 8), 8)
        for four in range(8):
            for v in range(2):
                shifts = []
                for j in range(2):
                    spread = flat[v, j * 8 + four, rows, :]
                    spread = jnp.where(bit0, pltpu.roll(spread, 32, 1), spread)
                    spread = jnp.where(bit1, pltpu.roll(spread, 64, 1), spread)
                    shifts.append(
                        [spread] + [pltpu.roll(spread, 128 - 32 * p, 1) for p in range(1, 4)]
                    )
                for p in range(4):
                    at = (four * 4 + p) * 32 + v * 16
                    for half in range(2):
                        block = jnp.concatenate([shifts[j][p] * masks[half] for j in range(2)], axis=0)
                        lhs[at : at + 16, half * 128 : half * 128 + 128] = block.astype(BF16)

    @pl.when(step == 0)
    def _():
        wide[0:2048] = spec[...].astype(F32)

        def turn(q, carry):
            j, four = q // 8, q % 8
            straight, crossed = [], []
            for p in range(4):
                row = lax.rem(four * 4 + p + 32 - lag[0], 32) * 8 + j
                got = [wide[pl.ds(row + 2 * r, 8, stride=256), :] for r in range(4)]
                straight += [got[0], got[1], -got[2], -got[3]]
                crossed += [got[2], got[3], got[0], got[1]]
            flat[0, q] = jnp.concatenate(straight, axis=0).T
            flat[1, q] = jnp.concatenate(crossed, axis=0).T
            return carry

        lax.fori_loop(0, 16, turn, 0, unroll=4)
    for group in range(2):
        spread_out(step * 16 + group * 8, (left, right)[group])
    for n in range(4):
        cols = pl.ds(n * 256, 256)
        powers = []
        for group in range(2):
            amp = dot((left, right)[group][...], w[group, :, cols])
            powers.append(jnp.sum((amp * amp).reshape(32, 4, 8, 256), axis=1))
        both = jnp.concatenate(powers, axis=1) * (1.0 / INPUTS)
        out[:, 0, :, cols] = both.astype(BF16)


def beams_of(lag, spec, w, chan_here):
    count = w.shape[2]
    return pl.pallas_call(
        beam_kernel,
        grid=(chan_here // 16,),
        in_specs=[
            pl.BlockSpec(memory_space=pltpu.SMEM),
            pl.BlockSpec(memory_space=pltpu.VMEM),
            pl.BlockSpec((2, 256, count), lambda k: (k, 0, 0)),
        ],
        out_specs=pl.BlockSpec((32, 1, 16, count), lambda k: (0, 0, k, 0)),
        out_shape=jax.ShapeDtypeStruct((32, 1, chan_here, count), BF16),
        scratch_shapes=[
            pltpu.VMEM((2304, LANES), F32),
            pltpu.VMEM((2, 16, LANES, LANES), F32),
            pltpu.VMEM((1024, 256), BF16),
            pltpu.VMEM((1024, 256), BF16),
        ],
        compiler_params=pltpu.CompilerParams(vmem_limit_bytes=40 << 20),
        cost_estimate=pl.CostEstimate(flops=9_000_000_000, bytes_accessed=17_000_000, transcendentals=0),
        name="beams",
    )(lag, spec, w)


def per_device(voltages, eq_gain, delays):
    frames = voltages.reshape(2, 16, INNER, LANES)
    count = lax.axis_size("shard")
    shard = lax.axis_index("shard")
    before = lax.ppermute(frames[:, 9:], "shard", [(at, at + 1) for at in range(count - 1)])
    after = lax.ppermute(frames[:, :8], "shard", [(at, (at - 1) % count) for at in range(count)])
    keep = jnp.where(shard == count - 1, 0.0, 1.0).astype(F32).reshape(1)
    chan_here = CHANNELS // count
    base, turn, gain = lax.optimization_barrier(
        (*angles(delays, shard * chan_here), eq_gain.reshape(2, 32, LANES))
    )
    messages = front(keep, before, frames, after, gain)
    got = lax.all_to_all(
        messages.reshape(256, 8, LANES), ("grp", "shard"), split_axis=0, concat_axis=0, tiled=True
    )
    w = pltpu.with_memory_space_constraint(weights(base, turn, chan_here), pltpu.HBM)
    lag = jnp.where(lax.axis_index("grp") < 4, 1, 0).astype(jnp.int32).reshape(1)
    return beams_of(lag, got.reshape(2048, LANES), w, chan_here)


def solution(mesh):
    placed = (P("grp", "shard"), P("grp", None), P())
    return jax.shard_map(
        per_device,
        mesh=mesh,
        in_specs=placed,
        out_specs=P(None, "grp", "shard", None),
        check_vma=False,
    )
```

time: 83.2 us -> 75.1 us (0.903)
  Pallas kernels: 34.1 us -> 28.5 us
  starting transfers between devices: 26.9 us -> 24.4 us
  local copies, waits for them, and re-layouts: 4.38 us -> 2.16 us
  other arithmetic: 1.34 us -> 2.63 us
    pallas_call x2, Pallas kernels: 16.2 us -> 11.8 us  [the longest x1 6.28 us: weights(): pl.pallas_call(weight_kernel, grid=(groups // 2,), in_specs=[whole, whole...]
    all_to_all x1, waiting for transfers between devices: 11.7 us -> 14.7 us  [per_device(): lax.all_to_all(messages.reshape(256, 8, LANES), ('grp', 'shard'), split_a...]
    all_to_all x1, starting transfers between devices: 22.3 us -> 19.8 us  [per_device(): lax.all_to_all(messages.reshape(256, 8, LANES), ('grp', 'shard'), split_a...]
    ppermute x1 -> x2, waiting for transfers between devices: 4.38 us -> 2.09 us  [the longest x1 2.09 us: per_device(): lax.ppermute(frames[:, :8], 'shard', [(at, (at - 1) % count) for at in ra...]
    unnamed x8 -> x2, local copies, waits for them, and re-layouts: 4.09 us -> 1.87 us
    another operation x2, other arithmetic: 0.02 us -> 1.31 us  [the longest x1 0.66 us: angles(): turn = jnp.stack([jnp.cos(step), -jnp.sin(step)])]
    pallas_call x1, Pallas kernels: 17.9 us -> 16.7 us  [beams_of(): pl.pallas_call(beam_kernel, grid=(chan_here // 16,), in_specs=[pl.BlockSp...]
    ppermute x1 -> x2, starting transfers between devices: 4.59 us -> 4.68 us  [the longest x1 4.59 us: per_device(): lax.ppermute(frames[:, 9:], 'shard', [(at, at + 1) for at in range(count...]
  transfers between devices with their start and end apart: 2 -> 3, of which waited for: 2 -> 2; matrix products, arithmetic and copies ran while one was open for 4% -> 5% of each run, Pallas kernels for 9% -> 8%
where the time goes in v2:
time: 75.1 us; the launch traced here: 74.6 us
  Pallas kernels  28.5 us (38%)
  starting transfers between devices  24.4 us (32%)
  waiting for transfers between devices  16.8 us (22%)
  other arithmetic  2.63 us (4%)
  local copies, waits for them, and re-layouts  2.16 us (3%)
    all_to_all x1, starting transfers between devices, per_device(): lax.all_to_all(messages.reshape(256, 8, LANES), ('grp', 'shard'), split_a...  19.8 us
    pallas_call x1, Pallas kernels, beams_of(): pl.pallas_call(beam_kernel, grid=(chan_here // 16,), in_specs=[pl.BlockSp...  16.7 us
    all_to_all x1, waiting for transfers between devices, per_device(): lax.all_to_all(messages.reshape(256, 8, LANES), ('grp', 'shard'), split_a...  14.7 us
    pallas_call x1, Pallas kernels, weights(): pl.pallas_call(weight_kernel, grid=(groups // 2,), in_specs=[whole, whole...  6.28 us
    pallas_call x1, Pallas kernels, front(): pl.pallas_call(front_kernel, in_specs=[pl.BlockSpec(memory_space=pltpu.SM...  5.53 us
    ppermute x1, starting transfers between devices, per_device(): lax.ppermute(frames[:, 9:], 'shard', [(at, at + 1) for at in range(count...  4.59 us
    ppermute x1, waiting for transfers between devices, per_device(): lax.ppermute(frames[:, :8], 'shard', [(at, (at - 1) % count) for at in ra...  2.09 us
    unnamed x2, local copies, waits for them, and re-layouts  1.87 us
  transfers between devices with their start and end apart: 3, of which 2 were waited for; matrix products, arithmetic and copies ran while one was open for 5% of the time, Pallas kernels for 8%

profile of v2, /device:TPU:1, one launch (start us, length us, event | category | flops | bytes accessed | tf_op | source)
XLA Modules:
  0.0 74.6 jit_solution(7019918999084062160)
XLA Ops:
  0.0 1.1 %copy.12 = bf16[1,2,1024,128]{3,2,1,0:T(8,128)(2,1)S(1)} copy(bf16[1,2,1024,128]{3,1,2,0:T(2,128)(2,1)} %bitcast.40) | data formatting | bytes 1048576
  1.1 4.6 %collective-permute-start = (bf16[2,7,64,128]{3,2,1,0:T(8,128)(2,1)S(1)}, bf16[2,7,64,128]{3,2,1,0:T(8,128)(2,1)S(1)}, u32[]{:S(2)}, u32[]{:S(2)}) collective-permute-start(bf16[2,7,64,128]{3,2,1,0:T(8,128)(2,1)S(1)} %slice.8), channel_id=1, source_target_pairs={{0,1},{1,2},{2,3},{3,4},{4,5},{5,6},{6,7},{7,8},{8,9},{9,10},{10,1... | collective-permute-start | bytes 688136 | tf_op jit(solution)/shard_map/ppermute | solution.py:315
  5.8 0.1 collective-permute-start.1
  5.9 1.3 %multiply_cosine_fusion = (f32[1024,16]{0,1:T(8,128)S(1)}, f32[1024,16]{0,1:T(8,128)S(1)}, f32[1024,16]{0,1:T(8,128)S(1)}, f32[1024,16]{0,1:T(8,128)S(1)}) fusion(f32[1024,16]{0,1:T(8,128)} %param.9, f32[]{:T(128)S(6)} %add.3), kind=kLoop, calls=%fused_computation.9 | loop fusion | flops 81920 | bytes 327684 | tf_op jit(solution)/shard_map/cos | solution.py:212
  7.5 0.8 %copy.19 = f32[1,2,32,128]{3,2,1,0:T(8,128)S(1)} copy(f32[1,2,32,128]{3,1,2,0:T(2,128)} %bitcast.41) | data formatting | bytes 65536
  8.2 0.7 pad_maximum_fusion.1.turn
  8.9 0.7 pad_maximum_fusion.base
  9.6 0.0 collective-permute-done.before
  9.6 2.1 %collective-permute-done.1.after = bf16[2,8,64,128]{3,2,1,0:T(8,128)(2,1)S(1)} collective-permute-done((bf16[2,8,64,128]{3,2,1,0:T(8,128)(2,1)S(1)}, bf16[2,8,64,128]{3,2,1,0:T(8,128)(2,1)S(1)}, u32[]{:S(2)}, u32[]{:S(2)}) %collective-permute-start.1) | collective-permute-done | bytes 262176 | tf_op jit(solution)/shard_map/ppermute | solution.py:316
  11.6 5.5 %front.1 = bf16[8,256,128]{2,1,0:T(8,128)(2,1)} custom-call(f32[1]{0:T(128)} %bitcast.1.keep, bf16[2,7,64,128]{3,2,1,0:T(8,128)(2,1)S(1)} %collective-permute-done.before, bf16[2,16,64,128]{3,2,1,0:T(8,128)(2,1)S(1)} %bitcast.37, bf16[2,8,64,128]{3,2,1,0:T(8,128)(2,1)S(1)} %collective-permute-done.1.after, f32[16,64,128]{2,1,0:T(8,128)} %constant.38.clone.win_far, ...), custom_call_target="tpu_custom_call" | custom-call | flops 400000000 | bytes 3000000 | tf_op jit(solution)/shard_map/front/pallas_call | solution.py:164
  17.2 19.8 %all-to-all-start = ((bf16[256,8,128]{2,1,0:T(8,128)(2,1)}), bf16[256,8,128]{2,1,0:T(8,128)(2,1)S(1)}, u32[]{:S(2)}, u32[]{:S(2)}) async-start(bf16[256,8,128]{2,1,0:T(8,128)(2,1)} %bitcast.10), calls=%async_computation | async-start | bytes 1048576 | tf_op jit(solution)/shard_map/all_to_all | solution.py:323
  37.0 6.3 %weights.1.w = bf16[16,256,1024]{2,1,0:T(8,128)(2,1)} custom-call(f32[2,16,1024]{2,1,0:T(8,128)} %pad_maximum_fusion.base, f32[2,16,1024]{2,1,0:T(8,128)} %pad_maximum_fusion.1.turn), custom_call_target="tpu_custom_call" | custom-call | flops 20000000 | bytes 9000000 | tf_op jit(solution)/shard_map/weights/pallas_call | solution.py:220
  43.2 14.7 %all-to-all-done = bf16[256,8,128]{2,1,0:T(8,128)(2,1)S(1)} async-done(((bf16[256,8,128]{2,1,0:T(8,128)(2,1)}), bf16[256,8,128]{2,1,0:T(8,128)(2,1)S(1)}, u32[]{:S(2)}, u32[]{:S(2)}) %all-to-all-start) | async-done | bytes 524320 | tf_op jit(solution)/shard_map/all_to_all | solution.py:323
  58.0 16.7 %beams.1 = bf16[32,1,128,1024]{3,2,1,0:T(8,128)(2,1)} custom-call(s32[1]{0:T(128)} %bitcast.lag, bf16[2048,128]{1,0:T(8,128)(2,1)S(1)} %bitcast.38, bf16[16,256,1024]{2,1,0:T(8,128)(2,1)} %weights.1.w), custom_call_target="tpu_custom_call" | custom-call | flops 8999999488 | bytes 17000000 | tf_op jit(solution)/shard_map/beams/pallas_call | solution.py:289
  (8 shorter events, 0.3 us)
Async XLA Ops:
  1.1 8.4 %collective-permute-start = (bf16[2,7,64,128]{3,2,1,0:T(8,128)(2,1)S(1)}, bf16[2,7,64,128]{3,2,1,0:T(8,128)(2,1)S(1)}, u32[]{:S(2)}, u32[]{:S(2)}) collective-permute-start(bf16[2,7,64,128]{3,2,1,0:T(8,128)(2,1)S(1)} %slice.8), channel_id=1, source_target_pairs={{0,1},{1,2},{2,3},{3,4},{4,5},{5,6},{6,7},{7,8},{8,9},{9,10},{10,1... | collective-permute-start | bytes 688136 | tf_op jit(solution)/shard_map/ppermute | solution.py:315
  5.8 5.9 %collective-permute-start.1 = (bf16[2,8,64,128]{3,2,1,0:T(8,128)(2,1)S(1)}, bf16[2,8,64,128]{3,2,1,0:T(8,128)(2,1)S(1)}, u32[]{:S(2)}, u32[]{:S(2)}) collective-permute-start(bf16[2,8,64,128]{3,2,1,0:T(8,128)(2,1)S(1)} %slice.9), channel_id=1, source_target_pairs={{0,31},{1,0},{2,1},{3,2},{4,3},{5,4},{6,5},{7,6},{8,7},{9,8},{10,9... | collective-permute-start | bytes 786440 | tf_op jit(solution)/shard_map/ppermute | solution.py:316
  17.2 40.8 %all-to-all-start = ((bf16[256,8,128]{2,1,0:T(8,128)(2,1)}), bf16[256,8,128]{2,1,0:T(8,128)(2,1)S(1)}, u32[]{:S(2)}, u32[]{:S(2)}) async-start(bf16[256,8,128]{2,1,0:T(8,128)(2,1)} %bitcast.10), calls=%async_computation | async-start | bytes 1048576 | tf_op jit(solution)/shard_map/all_to_all | solution.py:323

commit v3 on v2

--- a/solution.py
+++ b/solution.py
@@ -52,7 +52,7 @@
     cos, sin = np.cos(phase), np.sin(phase)
     from_real = np.stack([cos, -sin], axis=2).reshape(LANES, LANES)
     from_imag = np.stack([sin, cos], axis=2).reshape(LANES, LANES)
-    return np.stack(split(np.concatenate([from_real, from_imag], axis=0)))
+    return split(np.concatenate([from_real, from_imag], axis=0))[0]
 
 
 def dot(left, right):
@@ -123,8 +123,7 @@
             turned.append(
                 jnp.concatenate([re * t_re - im * t_im, re * t_im + im * t_re], axis=1)
             )
-        high, low = parts_of(jnp.concatenate(turned, axis=0))
-        spec = dot(high, second[0]) + dot(low, second[0]) + dot(high, second[1])
+        spec = dot(jnp.concatenate(turned, axis=0).astype(BF16), second[...])
         for i in range(2):
             flipped = spec[i * 128 : i * 128 + 128].T
             even, odd = flipped[:64], flipped[64:]
@@ -175,7 +174,7 @@
             pltpu.VMEM((TAPS, INNER, LANES), F32),
             pltpu.VMEM((128, 192), BF16),
             pltpu.VMEM((2, INNER, LANES), F32),
-            pltpu.VMEM((2, 256, LANES), BF16),
+            pltpu.VMEM((256, LANES), BF16),
             pltpu.SemaphoreType.DMA((4,)),
         ],
         compiler_params=pltpu.CompilerParams(vmem_limit_bytes=24 << 20),
@@ -230,7 +229,7 @@
     )(base, turn)
 
 
-def beam_kernel(lag, spec, w, out, wide, flat, left, right):
+def beam_kernel(lag, spec, w, out, wide, flat, left, right, l2, l3):
     step = pl.program_id(0)
     lane = lax.broadcasted_iota(jnp.int32, (8, LANES), 1) // 32
     chan = lax.broadcasted_iota(jnp.int32, (8, LANES), 0)
@@ -271,34 +270,42 @@
             flat[1, q] = jnp.concatenate(crossed, axis=0).T
             return carry
 
-        lax.fori_loop(0, 16, turn, 0, unroll=4)
-    for group in range(2):
-        spread_out(step * 16 + group * 8, (left, right)[group])
-    for n in range(4):
-        cols = pl.ds(n * 256, 256)
-        powers = []
-        for group in range(2):
-            amp = dot((left, right)[group][...], w[group, :, cols])
-            powers.append(jnp.sum((amp * amp).reshape(32, 4, 8, 256), axis=1))
-        both = jnp.concatenate(powers, axis=1) * (1.0 / INPUTS)
-        out[:, 0, :, cols] = both.astype(BF16)
+        lax.fori_loop(0, 16, turn, 0, unroll=16)
+    def form(pair, refs):
+        for n in range(4):
+            cols = pl.ds(n * 256, 256)
+            powers = []
+            for group in range(2):
+                amp = dot(refs[group][...], w[pair * 2 + group, :, cols])
+                powers.append(jnp.sum((amp * amp).reshape(32, 4, 8, 256), axis=1))
+            both = jnp.concatenate(powers, axis=1) * (1.0 / INPUTS)
+            out[:, 0, pair * 16 : pair * 16 + 16, cols] = both.astype(BF16)
+
+    spread_out(step * 32 + 0, left)
+    spread_out(step * 32 + 8, right)
+    form(0, (left, right))
+    spread_out(step * 32 + 16, l2)
+    spread_out(step * 32 + 24, l3)
+    form(1, (l2, l3))
 
 
 def beams_of(lag, spec, w, chan_here):
     count = w.shape[2]
     return pl.pallas_call(
         beam_kernel,
-        grid=(chan_here // 16,),
+        grid=(chan_here // 32,),
         in_specs=[
             pl.BlockSpec(memory_space=pltpu.SMEM),
             pl.BlockSpec(memory_space=pltpu.VMEM),
-            pl.BlockSpec((2, 256, count), lambda k: (k, 0, 0)),
+            pl.BlockSpec((4, 256, count), lambda k: (k, 0, 0)),
         ],
-        out_specs=pl.BlockSpec((32, 1, 16, count), lambda k: (0, 0, k, 0)),
+        out_specs=pl.BlockSpec((32, 1, 32, count), lambda k: (0, 0, k, 0)),
         out_shape=jax.ShapeDtypeStruct((32, 1, chan_here, count), BF16),
         scratch_shapes=[
             pltpu.VMEM((2304, LANES), F32),
             pltpu.VMEM((2, 16, LANES, LANES), F32),
+            pltpu.VMEM((1024, 256), BF16),
+            pltpu.VMEM((1024, 256), BF16),
             pltpu.VMEM((1024, 256), BF16),
             pltpu.VMEM((1024, 256), BF16),
         ],

time: 75.1 us -> 71.9 us (0.957)
  Pallas kernels: 28.5 us -> 25.4 us
    pallas_call x1, Pallas kernels: 16.7 us -> 14.8 us  [beams_of(): pl.pallas_call(beam_kernel, grid=(chan_here // 32,), in_specs=[pl.BlockSp...]
    pallas_call x1, Pallas kernels: 5.53 us -> 4.34 us  [front(): pl.pallas_call(front_kernel, in_specs=[pl.BlockSpec(memory_space=pltpu.SM...]
  transfers between devices with their start and end apart: 3 -> 3, of which waited for: 2 -> 2; matrix products, arithmetic and copies ran while one was open for 5% -> 5% of each run, Pallas kernels for 8% -> 9%
where the time goes in v3:
time: 71.9 us; the launch traced here: 71.5 us
  Pallas kernels  25.4 us (35%)
  starting transfers between devices  24.4 us (34%)
  waiting for transfers between devices  16.8 us (23%)
  other arithmetic  2.63 us (4%)
  local copies, waits for them, and re-layouts  2.16 us (3%)
    all_to_all x1, starting transfers between devices, per_device(): lax.all_to_all(messages.reshape(256, 8, LANES), ('grp', 'shard'), split_a...  19.8 us
    pallas_call x1, Pallas kernels, beams_of(): pl.pallas_call(beam_kernel, grid=(chan_here // 32,), in_specs=[pl.BlockSp...  14.8 us
    all_to_all x1, waiting for transfers between devices, per_device(): lax.all_to_all(messages.reshape(256, 8, LANES), ('grp', 'shard'), split_a...  14.7 us
    pallas_call x1, Pallas kernels, weights(): pl.pallas_call(weight_kernel, grid=(groups // 2,), in_specs=[whole, whole...  6.28 us
    ppermute x1, starting transfers between devices, per_device(): lax.ppermute(frames[:, 9:], 'shard', [(at, at + 1) for at in range(count...  4.59 us
    pallas_call x1, Pallas kernels, front(): pl.pallas_call(front_kernel, in_specs=[pl.BlockSpec(memory_space=pltpu.SM...  4.34 us
    ppermute x1, waiting for transfers between devices, per_device(): lax.ppermute(frames[:, :8], 'shard', [(at, (at - 1) % count) for at in ra...  2.09 us
    unnamed x2, local copies, waits for them, and re-layouts  1.87 us
  transfers between devices with their start and end apart: 3, of which 2 were waited for; matrix products, arithmetic and copies ran while one was open for 5% of the time, Pallas kernels for 9%

profile of v3, /device:TPU:1, one launch (start us, length us, event | category | flops | bytes accessed | tf_op | source)
XLA Modules:
  0.0 71.5 jit_solution(12025594935462144424)
XLA Ops:
  0.0 1.1 %copy.12 = bf16[1,2,1024,128]{3,2,1,0:T(8,128)(2,1)S(1)} copy(bf16[1,2,1024,128]{3,1,2,0:T(2,128)(2,1)} %bitcast.40) | data formatting | bytes 1048576
  1.1 4.6 %collective-permute-start = (bf16[2,7,64,128]{3,2,1,0:T(8,128)(2,1)S(1)}, bf16[2,7,64,128]{3,2,1,0:T(8,128)(2,1)S(1)}, u32[]{:S(2)}, u32[]{:S(2)}) collective-permute-start(bf16[2,7,64,128]{3,2,1,0:T(8,128)(2,1)S(1)} %slice.8), channel_id=1, source_target_pairs={{0,1},{1,2},{2,3},{3,4},{4,5},{5,6},{6,7},{7,8},{8,9},{9,10},{10,1... | collective-permute-start | bytes 688136 | tf_op jit(solution)/shard_map/ppermute | solution.py:322
  5.8 0.1 collective-permute-start.1
  5.9 1.3 %multiply_cosine_fusion = (f32[1024,16]{0,1:T(8,128)S(1)}, f32[1024,16]{0,1:T(8,128)S(1)}, f32[1024,16]{0,1:T(8,128)S(1)}, f32[1024,16]{0,1:T(8,128)S(1)}) fusion(f32[1024,16]{0,1:T(8,128)} %param.9, f32[]{:T(128)S(6)} %add.3), kind=kLoop, calls=%fused_computation.9 | loop fusion | flops 81920 | bytes 327684 | tf_op jit(solution)/shard_map/cos | solution.py:211
  7.5 0.8 %copy.19 = f32[1,2,32,128]{3,2,1,0:T(8,128)S(1)} copy(f32[1,2,32,128]{3,1,2,0:T(2,128)} %bitcast.41) | data formatting | bytes 65536
  8.2 0.7 pad_maximum_fusion.1.turn
  8.9 0.7 pad_maximum_fusion.base
  9.6 0.0 collective-permute-done.before
  9.6 2.1 %collective-permute-done.1.after = bf16[2,8,64,128]{3,2,1,0:T(8,128)(2,1)S(1)} collective-permute-done((bf16[2,8,64,128]{3,2,1,0:T(8,128)(2,1)S(1)}, bf16[2,8,64,128]{3,2,1,0:T(8,128)(2,1)S(1)}, u32[]{:S(2)}, u32[]{:S(2)}) %collective-permute-start.1) | collective-permute-done | bytes 262176 | tf_op jit(solution)/shard_map/ppermute | solution.py:323
  11.6 4.3 %front.1 = bf16[8,256,128]{2,1,0:T(8,128)(2,1)} custom-call(f32[1]{0:T(128)} %bitcast.1.keep, bf16[2,7,64,128]{3,2,1,0:T(8,128)(2,1)S(1)} %collective-permute-done.before, bf16[2,16,64,128]{3,2,1,0:T(8,128)(2,1)S(1)} %bitcast.37, bf16[2,8,64,128]{3,2,1,0:T(8,128)(2,1)S(1)} %collective-permute-done.1.after, f32[16,64,128]{2,1,0:T(8,128)} %constant.38.clone.win_far, ...), custom_call_target="tpu_custom_call" | custom-call | flops 400000000 | bytes 3000000 | tf_op jit(solution)/shard_map/front/pallas_call | solution.py:163
  16.0 19.8 %all-to-all-start = ((bf16[256,8,128]{2,1,0:T(8,128)(2,1)}), bf16[256,8,128]{2,1,0:T(8,128)(2,1)S(1)}, u32[]{:S(2)}, u32[]{:S(2)}) async-start(bf16[256,8,128]{2,1,0:T(8,128)(2,1)} %bitcast.10), calls=%async_computation | async-start | bytes 1048576 | tf_op jit(solution)/shard_map/all_to_all | solution.py:330
  35.8 6.3 %weights.1.w = bf16[16,256,1024]{2,1,0:T(8,128)(2,1)} custom-call(f32[2,16,1024]{2,1,0:T(8,128)} %pad_maximum_fusion.base, f32[2,16,1024]{2,1,0:T(8,128)} %pad_maximum_fusion.1.turn), custom_call_target="tpu_custom_call" | custom-call | flops 20000000 | bytes 9000000 | tf_op jit(solution)/shard_map/weights/pallas_call | solution.py:219
  42.0 14.7 %all-to-all-done = bf16[256,8,128]{2,1,0:T(8,128)(2,1)S(1)} async-done(((bf16[256,8,128]{2,1,0:T(8,128)(2,1)}), bf16[256,8,128]{2,1,0:T(8,128)(2,1)S(1)}, u32[]{:S(2)}, u32[]{:S(2)}) %all-to-all-start) | async-done | bytes 524320 | tf_op jit(solution)/shard_map/all_to_all | solution.py:330
  56.8 14.8 %beams.1 = bf16[32,1,128,1024]{3,2,1,0:T(8,128)(2,1)} custom-call(s32[1]{0:T(128)} %bitcast.lag, bf16[2048,128]{1,0:T(8,128)(2,1)S(1)} %bitcast.38, bf16[16,256,1024]{2,1,0:T(8,128)(2,1)} %weights.1.w), custom_call_target="tpu_custom_call" | custom-call | flops 8999999488 | bytes 17000000 | tf_op jit(solution)/shard_map/beams/pallas_call | solution.py:294
  (8 shorter events, 0.3 us)
Async XLA Ops:
  1.1 8.4 %collective-permute-start = (bf16[2,7,64,128]{3,2,1,0:T(8,128)(2,1)S(1)}, bf16[2,7,64,128]{3,2,1,0:T(8,128)(2,1)S(1)}, u32[]{:S(2)}, u32[]{:S(2)}) collective-permute-start(bf16[2,7,64,128]{3,2,1,0:T(8,128)(2,1)S(1)} %slice.8), channel_id=1, source_target_pairs={{0,1},{1,2},{2,3},{3,4},{4,5},{5,6},{6,7},{7,8},{8,9},{9,10},{10,1... | collective-permute-start | bytes 688136 | tf_op jit(solution)/shard_map/ppermute | solution.py:322
  5.8 5.9 %collective-permute-start.1 = (bf16[2,8,64,128]{3,2,1,0:T(8,128)(2,1)S(1)}, bf16[2,8,64,128]{3,2,1,0:T(8,128)(2,1)S(1)}, u32[]{:S(2)}, u32[]{:S(2)}) collective-permute-start(bf16[2,8,64,128]{3,2,1,0:T(8,128)(2,1)S(1)} %slice.9), channel_id=1, source_target_pairs={{0,31},{1,0},{2,1},{3,2},{4,3},{5,4},{6,5},{7,6},{8,7},{9,8},{10,9... | collective-permute-start | bytes 786440 | tf_op jit(solution)/shard_map/ppermute | solution.py:323
  16.0 40.8 %all-to-all-start = ((bf16[256,8,128]{2,1,0:T(8,128)(2,1)}), bf16[256,8,128]{2,1,0:T(8,128)(2,1)S(1)}, u32[]{:S(2)}, u32[]{:S(2)}) async-start(bf16[256,8,128]{2,1,0:T(8,128)(2,1)} %bitcast.10), calls=%async_computation | async-start | bytes 1048576 | tf_op jit(solution)/shard_map/all_to_all | solution.py:330

commit v4 on v3

--- a/solution.py
+++ b/solution.py
@@ -72,7 +72,7 @@
 
 
 def front_kernel(
-    keep, before, own, after, win_far, first_far, twist_far, second_far, gain, out,
+    place, keep, far_side, own, near_side, win_far, first_far, twist_far, second_far, gain, out,
     wide, flt, inter, win, first, twist, second, arrived,
 ):
     tables = ((win_far, win), (first_far, first), (twist_far, twist), (second_far, second))
@@ -82,9 +82,20 @@
     for copy in copies:
         copy.start()
     for i in range(2):
-        wide[i, 0:7] = before[i].astype(F32)
         wide[i, 7:23] = own[i].astype(F32)
-        wide[i, 23:31] = after[i].astype(F32)
+
+    @pl.when(place[0] == 0)
+    def _():
+        for i in range(2):
+            wide[i, 0:7] = far_side[i, 1:8].astype(F32)
+            wide[i, 23:31] = near_side[i].astype(F32)
+
+    @pl.when(place[0] != 0)
+    def _():
+        for i in range(2):
+            wide[i, 0:7] = near_side[i, 1:8].astype(F32)
+            wide[i, 23:31] = far_side[i].astype(F32)
+
     keep_old = keep[0]
     for copy in copies:
         copy.wait()
@@ -148,12 +159,13 @@
     return pltpu.with_memory_space_constraint(jnp.asarray(table), pltpu.HBM)
 
 
-def front(keep, before, own, after, gain):
+def front(place, keep, far_side, own, near_side, gain):
     args = (
+        place,
         keep,
-        before,
+        far_side,
         own,
-        after,
+        near_side,
         far(window_table()),
         far(first_table()),
         far(twist_table()),
@@ -162,7 +174,7 @@
     )
     return pl.pallas_call(
         front_kernel,
-        in_specs=[pl.BlockSpec(memory_space=pltpu.SMEM)]
+        in_specs=[pl.BlockSpec(memory_space=pltpu.SMEM)] * 2
         + [pl.BlockSpec(memory_space=pltpu.VMEM)] * 3
         + [pl.BlockSpec(memory_space=pltpu.HBM)] * 4
         + [pl.BlockSpec(memory_space=pltpu.VMEM)],
@@ -271,6 +283,7 @@
             return carry
 
         lax.fori_loop(0, 16, turn, 0, unroll=16)
+
     def form(pair, refs):
         for n in range(4):
             cols = pl.ds(n * 256, 256)
@@ -281,7 +294,7 @@
             both = jnp.concatenate(powers, axis=1) * (1.0 / INPUTS)
             out[:, 0, pair * 16 : pair * 16 + 16, cols] = both.astype(BF16)
 
-    spread_out(step * 32 + 0, left)
+    spread_out(step * 32, left)
     spread_out(step * 32 + 8, right)
     form(0, (left, right))
     spread_out(step * 32 + 16, l2)
@@ -319,14 +332,20 @@
     frames = voltages.reshape(2, 16, INNER, LANES)
     count = lax.axis_size("shard")
     shard = lax.axis_index("shard")
-    before = lax.ppermute(frames[:, 9:], "shard", [(at, at + 1) for at in range(count - 1)])
-    after = lax.ppermute(frames[:, :8], "shard", [(at, (at - 1) % count) for at in range(count)])
+    place = shard % 2
+    halves = frames.reshape(2, 2, 8, INNER, LANES)
+    outer = lax.dynamic_index_in_dim(halves, place, 1, keepdims=False)
+    inner = lax.dynamic_index_in_dim(halves, 1 - place, 1, keepdims=False)
+    swaps = [(at, (at - 1) % count) for at in range(0, count, 2)]
+    far_side = lax.ppermute(outer, "shard", swaps + [(at, at + 1) for at in range(1, count - 1, 2)])
+    near_side = lax.ppermute(inner, "shard", [(at, at ^ 1) for at in range(count)])
     keep = jnp.where(shard == count - 1, 0.0, 1.0).astype(F32).reshape(1)
     chan_here = CHANNELS // count
     base, turn, gain = lax.optimization_barrier(
         (*angles(delays, shard * chan_here), eq_gain.reshape(2, 32, LANES))
     )
-    messages = front(keep, before, frames, after, gain)
+    place = place.astype(jnp.int32).reshape(1)
+    messages = front(place, keep, far_side, frames, near_side, gain)
     got = lax.all_to_all(
         messages.reshape(256, 8, LANES), ("grp", "shard"), split_axis=0, concat_axis=0, tiled=True
     )

time: 71.9 us -> 71.2 us (level)
    all_to_all x1, starting transfers between devices: 19.8 us -> 18.5 us  [per_device(): lax.all_to_all(messages.reshape(256, 8, LANES), ('grp', 'shard'), split_a...]
where the time goes in v4:
time: 71.2 us; the launch traced here: 70.8 us
  Pallas kernels  25.4 us (36%)
  starting transfers between devices  23.7 us (33%)
  waiting for transfers between devices  16.8 us (24%)
  other arithmetic  2.62 us (4%)
  local copies, waits for them, and re-layouts  2.17 us (3%)
    all_to_all x1, starting transfers between devices, per_device(): lax.all_to_all(messages.reshape(256, 8, LANES), ('grp', 'shard'), split_a...  18.5 us
    pallas_call x1, Pallas kernels, beams_of(): pl.pallas_call(beam_kernel, grid=(chan_here // 32,), in_specs=[pl.BlockSp...  14.8 us
    all_to_all x1, waiting for transfers between devices, per_device(): lax.all_to_all(messages.reshape(256, 8, LANES), ('grp', 'shard'), split_a...  14.7 us
    pallas_call x1, Pallas kernels, weights(): pl.pallas_call(weight_kernel, grid=(groups // 2,), in_specs=[whole, whole...  6.27 us
    pallas_call x1, Pallas kernels, front(): pl.pallas_call(front_kernel, in_specs=[pl.BlockSpec(memory_space=pltpu.SM...  4.34 us
    ppermute x1, starting transfers between devices, per_device(): lax.ppermute(inner, 'shard', [(at, at ^ 1) for at in range(count)])  3.33 us
    ppermute x1, waiting for transfers between devices, per_device(): lax.ppermute(outer, 'shard', swaps + [(at, at + 1) for at in range(1, cou...  2.08 us
    ppermute x1, starting transfers between devices, per_device(): lax.ppermute(outer, 'shard', swaps + [(at, at + 1) for at in range(1, cou...  1.91 us
  transfers between devices with their start and end apart: 3, of which 2 were waited for; matrix products, arithmetic and copies ran while one was open for 5% of the time, Pallas kernels for 9%

profile of v4, /device:TPU:1, one launch (start us, length us, event | category | flops | bytes accessed | tf_op | source)
XLA Modules:
  0.0 70.8 jit_solution(1655955445974091799)
XLA Ops:
  0.0 1.1 %copy.16 = bf16[1,2,1024,128]{3,2,1,0:T(8,128)(2,1)S(1)} copy(bf16[1,2,1024,128]{3,1,2,0:T(2,128)(2,1)} %bitcast.51) | data formatting | bytes 1048576
  1.2 3.3 %collective-permute-start.1 = (bf16[2,8,64,128]{3,2,1,0:T(8,128)(2,1)S(1)}, bf16[2,8,64,128]{3,2,1,0:T(8,128)(2,1)S(1)}, u32[]{:S(2)}, u32[]{:S(2)}) collective-permute-start(bf16[2,8,64,128]{3,2,1,0:T(8,128)(2,1)S(1)} %get-tuple-element.11), channel_id=1, source_target_pairs={{0,1},{1,0},{2,3},{3,2},{4,5},{5,4},{6,7},{7,6},{8,9},{9,8},{10,11... | collective-permute-start | bytes 786440 | tf_op jit(solution)/shard_map/ppermute | solution.py:341
  4.5 1.9 %collective-permute-start = (bf16[2,8,64,128]{3,2,1,0:T(8,128)(2,1)S(1)}, bf16[2,8,64,128]{3,2,1,0:T(8,128)(2,1)S(1)}, u32[]{:S(2)}, u32[]{:S(2)}) collective-permute-start(bf16[2,8,64,128]{3,2,1,0:T(8,128)(2,1)S(1)} %get-tuple-element.12), channel_id=1, source_target_pairs={{0,31},{2,1},{4,3},{6,5},{8,7},{10,9},{12,11},{14,13},{16,15},{18,... | collective-permute-start | bytes 786440 | tf_op jit(solution)/shard_map/ppermute | solution.py:340
  6.4 1.3 %multiply_cosine_fusion = (f32[1024,16]{0,1:T(8,128)S(1)}, f32[1024,16]{0,1:T(8,128)S(1)}, f32[1024,16]{0,1:T(8,128)S(1)}, f32[1024,16]{0,1:T(8,128)S(1)}) fusion(f32[1024,16]{0,1:T(8,128)} %param.9, f32[]{:T(128)S(6)} %add.18), kind=kLoop, calls=%fused_computation.11 | loop fusion | flops 81920 | bytes 327684 | tf_op jit(solution)/shard_map/cos | solution.py:223
  8.0 0.8 %copy.24 = f32[1,2,32,128]{3,2,1,0:T(8,128)S(1)} copy(f32[1,2,32,128]{3,1,2,0:T(2,128)} %bitcast.52) | data formatting | bytes 65536
  8.8 0.7 pad_maximum_fusion.1.turn
  9.5 0.6 pad_maximum_fusion.base
  10.1 0.0 collective-permute-done.1.near_side
  10.1 2.1 %collective-permute-done.far_side = bf16[2,8,64,128]{3,2,1,0:T(8,128)(2,1)S(1)} collective-permute-done((bf16[2,8,64,128]{3,2,1,0:T(8,128)(2,1)S(1)}, bf16[2,8,64,128]{3,2,1,0:T(8,128)(2,1)S(1)}, u32[]{:S(2)}, u32[]{:S(2)}) %collective-permute-start) | collective-permute-done | bytes 262176 | tf_op jit(solution)/shard_map/ppermute | solution.py:340
  12.2 4.3 %front.1 = bf16[8,256,128]{2,1,0:T(8,128)(2,1)} custom-call(s32[1]{0:T(128)} %bitcast.1.place, f32[1]{0:T(128)} %bitcast.2.keep, bf16[2,8,64,128]{3,2,1,0:T(8,128)(2,1)S(1)} %collective-permute-done.far_side, bf16[2,16,64,128]{3,2,1,0:T(8,128)(2,1)S(1)} %bitcast.48, bf16[2,8,64,128]{3,2,1,0:T(8,128)(2,1)S(1)} %collective-permute-done.1.near_side, ...), custom_call_target="tpu_custom_call" | custom-call | flops 400000000 | bytes 3000000 | tf_op jit(solution)/shard_map/front/pallas_call | solution.py:175
  16.5 18.5 %all-to-all-start = ((bf16[256,8,128]{2,1,0:T(8,128)(2,1)}), bf16[256,8,128]{2,1,0:T(8,128)(2,1)S(1)}, u32[]{:S(2)}, u32[]{:S(2)}) async-start(bf16[256,8,128]{2,1,0:T(8,128)(2,1)} %bitcast.13), calls=%async_computation | async-start | bytes 1048576 | tf_op jit(solution)/shard_map/all_to_all | solution.py:349
  35.0 6.3 %weights.1.w = bf16[16,256,1024]{2,1,0:T(8,128)(2,1)} custom-call(f32[2,16,1024]{2,1,0:T(8,128)} %pad_maximum_fusion.base, f32[2,16,1024]{2,1,0:T(8,128)} %pad_maximum_fusion.1.turn), custom_call_target="tpu_custom_call" | custom-call | flops 20000000 | bytes 9000000 | tf_op jit(solution)/shard_map/weights/pallas_call | solution.py:231
  41.3 14.7 %all-to-all-done = bf16[256,8,128]{2,1,0:T(8,128)(2,1)S(1)} async-done(((bf16[256,8,128]{2,1,0:T(8,128)(2,1)}), bf16[256,8,128]{2,1,0:T(8,128)(2,1)S(1)}, u32[]{:S(2)}, u32[]{:S(2)}) %all-to-all-start) | async-done | bytes 524320 | tf_op jit(solution)/shard_map/all_to_all | solution.py:349
  56.0 14.8 %beams.1 = bf16[32,1,128,1024]{3,2,1,0:T(8,128)(2,1)} custom-call(s32[1]{0:T(128)} %bitcast.lag, bf16[2048,128]{1,0:T(8,128)(2,1)S(1)} %bitcast.49, bf16[16,256,1024]{2,1,0:T(8,128)(2,1)} %weights.1.w), custom_call_target="tpu_custom_call" | custom-call | flops 8999999488 | bytes 17000000 | tf_op jit(solution)/shard_map/beams/pallas_call | solution.py:307
  (7 shorter events, 0.3 us)
Async XLA Ops:
  1.2 8.9 %collective-permute-start.1 = (bf16[2,8,64,128]{3,2,1,0:T(8,128)(2,1)S(1)}, bf16[2,8,64,128]{3,2,1,0:T(8,128)(2,1)S(1)}, u32[]{:S(2)}, u32[]{:S(2)}) collective-permute-start(bf16[2,8,64,128]{3,2,1,0:T(8,128)(2,1)S(1)} %get-tuple-element.11), channel_id=1, source_target_pairs={{0,1},{1,0},{2,3},{3,2},{4,5},{5,4},{6,7},{7,6},{8,9},{9,8},{10,11... | collective-permute-start | bytes 786440 | tf_op jit(solution)/shard_map/ppermute | solution.py:341
  4.5 7.7 %collective-permute-start = (bf16[2,8,64,128]{3,2,1,0:T(8,128)(2,1)S(1)}, bf16[2,8,64,128]{3,2,1,0:T(8,128)(2,1)S(1)}, u32[]{:S(2)}, u32[]{:S(2)}) collective-permute-start(bf16[2,8,64,128]{3,2,1,0:T(8,128)(2,1)S(1)} %get-tuple-element.12), channel_id=1, source_target_pairs={{0,31},{2,1},{4,3},{6,5},{8,7},{10,9},{12,11},{14,13},{16,15},{18,... | collective-permute-start | bytes 786440 | tf_op jit(solution)/shard_map/ppermute | solution.py:340
  16.5 39.5 %all-to-all-start = ((bf16[256,8,128]{2,1,0:T(8,128)(2,1)}), bf16[256,8,128]{2,1,0:T(8,128)(2,1)S(1)}, u32[]{:S(2)}, u32[]{:S(2)}) async-start(bf16[256,8,128]{2,1,0:T(8,128)(2,1)} %bitcast.13), calls=%async_computation | async-start | bytes 1048576 | tf_op jit(solution)/shard_map/all_to_all | solution.py:349

commit v5 on v4

--- a/solution.py
+++ b/solution.py
@@ -73,7 +73,7 @@
 
 def front_kernel(
     place, keep, far_side, own, near_side, win_far, first_far, twist_far, second_far, gain, out,
-    wide, flt, inter, win, first, twist, second, arrived,
+    wide, flt, inter, win, first, twist, second, arrived, ready, left,
 ):
     tables = ((win_far, win), (first_far, first), (twist_far, twist), (second_far, second))
     copies = [
@@ -81,6 +81,9 @@
     ]
     for copy in copies:
         copy.start()
+    sends = [
+        pltpu.make_async_copy(ready.at[g], out.at[(g + 4) % 8], left.at[g]) for g in range(8)
+    ]
     for i in range(2):
         wide[i, 7:23] = own[i].astype(F32)
 
@@ -148,11 +151,14 @@
                     inter[g, pl.ds(place, 32, stride=8), :] = (
                         rows[j][part * 32 : part * 32 + 32] * gain[i]
                     )
-        out[(g + 4) % 8] = inter[g, 0:256].astype(BF16)
+        ready[g] = inter[g, 0:256].astype(BF16)
+        sends[g].start()
         return carry
 
     for g in range(8):
         group_step(g, 0)
+    for send in sends:
+        send.wait()
 
 
 def far(table):
@@ -178,6 +184,7 @@
         + [pl.BlockSpec(memory_space=pltpu.VMEM)] * 3
         + [pl.BlockSpec(memory_space=pltpu.HBM)] * 4
         + [pl.BlockSpec(memory_space=pltpu.VMEM)],
+        out_specs=pl.BlockSpec(memory_space=pltpu.HBM),
         out_shape=jax.ShapeDtypeStruct((8, 256, LANES), BF16),
         scratch_shapes=[
             pltpu.VMEM((2, 31, INNER, LANES), F32),
@@ -188,6 +195,8 @@
             pltpu.VMEM((2, INNER, LANES), F32),
             pltpu.VMEM((256, LANES), BF16),
             pltpu.SemaphoreType.DMA((4,)),
+            pltpu.VMEM((8, 256, LANES), BF16),
+            pltpu.SemaphoreType.DMA((8,)),
         ],
         compiler_params=pltpu.CompilerParams(vmem_limit_bytes=24 << 20),
         cost_estimate=pl.CostEstimate(flops=400_000_000, bytes_accessed=3_000_000, transcendentals=0),
@@ -241,8 +250,15 @@
     )(base, turn)
 
 
-def beam_kernel(lag, spec, w, out, wide, flat, left, right, l2, l3):
+def beam_kernel(lag, spec, w_far, out, held, arrived, wide, flat, left, right, l2, l3):
     step = pl.program_id(0)
+    slot = lax.rem(step, 2)
+    w = held.at[slot]
+
+    def fetch(at, into):
+        blocks = w_far.at[pl.ds(at * 4, 4)]
+        return pltpu.make_async_copy(blocks, held.at[into], arrived.at[into])
+
     lane = lax.broadcasted_iota(jnp.int32, (8, LANES), 1) // 32
     chan = lax.broadcasted_iota(jnp.int32, (8, LANES), 0)
     bit0, bit1 = chan % 2 == 1, chan // 2 % 2 == 1
@@ -268,6 +284,7 @@
 
     @pl.when(step == 0)
     def _():
+        fetch(0, 0).start()
         wide[0:2048] = spec[...].astype(F32)
 
         def turn(q, carry):
@@ -284,6 +301,12 @@
 
         lax.fori_loop(0, 16, turn, 0, unroll=16)
 
+    @pl.when(step + 1 < pl.num_programs(0))
+    def _():
+        fetch(step + 1, 1 - slot).start()
+
+    fetch(step, slot).wait()
+
     def form(pair, refs):
         for n in range(4):
             cols = pl.ds(n * 256, 256)
@@ -310,11 +333,13 @@
         in_specs=[
             pl.BlockSpec(memory_space=pltpu.SMEM),
             pl.BlockSpec(memory_space=pltpu.VMEM),
-            pl.BlockSpec((4, 256, count), lambda k: (k, 0, 0)),
+            pl.BlockSpec(memory_space=pltpu.HBM),
         ],
         out_specs=pl.BlockSpec((32, 1, 32, count), lambda k: (0, 0, k, 0)),
         out_shape=jax.ShapeDtypeStruct((32, 1, chan_here, count), BF16),
         scratch_shapes=[
+            pltpu.VMEM((2, 4, 256, count), BF16),
+            pltpu.SemaphoreType.DMA((2,)),
             pltpu.VMEM((2304, LANES), F32),
             pltpu.VMEM((2, 16, LANES, LANES), F32),
             pltpu.VMEM((1024, 256), BF16),
@@ -334,7 +359,8 @@
     shard = lax.axis_index("shard")
     place = shard % 2
     halves = frames.reshape(2, 2, 8, INNER, LANES)
-    outer = lax.dynamic_index_in_dim(halves, place, 1, keepdims=False)
+    outer = lax.dynamic_slice_in_dim(voltages, place * (8 * LENGTH), 8 * LENGTH, 1)
+    outer = outer.reshape(2, 8, INNER, LANES)
     inner = lax.dynamic_index_in_dim(halves, 1 - place, 1, keepdims=False)
     swaps = [(at, (at - 1) % count) for at in range(0, count, 2)]
     far_side = lax.ppermute(outer, "shard", swaps + [(at, at + 1) for at in range(1, count - 1, 2)])

time: 71.2 us -> 70.2 us (0.986)
  waiting for transfers between devices: 16.8 us -> 14.7 us
  local copies, waits for them, and re-layouts: 2.17 us -> 3.32 us
    all_to_all x1, starting transfers between devices: 18.5 us -> 12.2 us  [per_device(): lax.all_to_all(messages.reshape(256, 8, LANES), ('grp', 'shard'), split_a...]
    ppermute x1, starting transfers between devices: 3.33 us -> 7.11 us  [per_device(): lax.ppermute(inner, 'shard', [(at, at ^ 1) for at in range(count)])]
    ppermute x1, starting transfers between devices: 1.91 us -> 4.59 us  [per_device(): lax.ppermute(outer, 'shard', swaps + [(at, at + 1) for at in range(1, cou...]
    ppermute x1, waiting for transfers between devices: 2.08 us -> 0.01 us  [per_device(): lax.ppermute(outer, 'shard', swaps + [(at, at + 1) for at in range(1, cou...]
    unnamed x2 -> x4, local copies, waits for them, and re-layouts: 1.87 us -> 3.04 us
  transfers between devices with their start and end apart: 3 -> 3, of which waited for: 2 -> 1; matrix products, arithmetic and copies ran while one was open for 5% -> 7% of each run, Pallas kernels for 9% -> 9%
where the time goes in v5:
time: 70.2 us; the launch traced here: 69.8 us
  Pallas kernels  25.2 us (36%)
  starting transfers between devices  23.9 us (34%)
  waiting for transfers between devices  14.7 us (21%)
  local copies, waits for them, and re-layouts  3.32 us (5%)
  other arithmetic  2.63 us (4%)
    all_to_all x1, waiting for transfers between devices, per_device(): lax.all_to_all(messages.reshape(256, 8, LANES), ('grp', 'shard'), split_a...  14.7 us
    pallas_call x1, Pallas kernels, beams_of(): pl.pallas_call(beam_kernel, grid=(chan_here // 32,), in_specs=[pl.BlockSp...  14.7 us
    all_to_all x1, starting transfers between devices, per_device(): lax.all_to_all(messages.reshape(256, 8, LANES), ('grp', 'shard'), split_a...  12.2 us
    ppermute x1, starting transfers between devices, per_device(): lax.ppermute(inner, 'shard', [(at, at ^ 1) for at in range(count)])  7.11 us
    pallas_call x1, Pallas kernels, weights(): pl.pallas_call(weight_kernel, grid=(groups // 2,), in_specs=[whole, whole...  6.28 us
    ppermute x1, starting transfers between devices, per_device(): lax.ppermute(outer, 'shard', swaps + [(at, at + 1) for at in range(1, cou...  4.59 us
    pallas_call x1, Pallas kernels, front(): pl.pallas_call(front_kernel, in_specs=[pl.BlockSpec(memory_space=pltpu.SM...  4.25 us
    unnamed x4, local copies, waits for them, and re-layouts  3.04 us
  transfers between devices with their start and end apart: 3, of which 1 were waited for; matrix products, arithmetic and copies ran while one was open for 7% of the time, Pallas kernels for 9%

profile of v5, /device:TPU:1, one launch (start us, length us, event | category | flops | bytes accessed | tf_op | source)
XLA Modules:
  0.0 69.8 jit_solution(4481283375746553969)
XLA Ops:
  0.0 1.1 %dynamic-slice_bitcast_fusion.1 = bf16[1,2,512,128]{3,1,2,0:T(2,128)(2,1)S(1)} fusion(bf16[2,131072]{1,0:T(2,128)(2,1)} %param.7, s32[]{:T(128)S(6)} %select_n.25), kind=kLoop, calls=%fused_computation.1 | loop fusion | bytes 524292
  1.2 4.6 %collective-permute-start = (bf16[2,8,64,128]{3,2,1,0:T(8,128)(2,1)S(1)}, bf16[2,8,64,128]{3,2,1,0:T(8,128)(2,1)S(1)}, u32[]{:S(2)}, u32[]{:S(2)}) collective-permute-start(bf16[2,8,64,128]{3,2,1,0:T(8,128)(2,1)S(1)} %bitcast.52), channel_id=1, source_target_pairs={{0,31},{2,1},{4,3},{6,5},{8,7},{10,9},{12,11},{14,13},{16,15},{18,... | collective-permute-start | bytes 786440 | tf_op jit(solution)/shard_map/ppermute | solution.py:366
  5.8 1.1 %copy.15 = bf16[1,2,1024,128]{3,2,1,0:T(8,128)(2,1)S(1)} copy(bf16[1,2,1024,128]{3,1,2,0:T(2,128)(2,1)} %bitcast.51) | data formatting | bytes 1048576
  6.9 7.1 %collective-permute-start.1 = (bf16[2,8,64,128]{3,2,1,0:T(8,128)(2,1)S(1)}, bf16[2,8,64,128]{3,2,1,0:T(8,128)(2,1)S(1)}, u32[]{:S(2)}, u32[]{:S(2)}) collective-permute-start(bf16[2,8,64,128]{3,2,1,0:T(8,128)(2,1)S(1)} %dynamic-slice_bitcast_fusion), channel_id=1, source_target_pairs={{0,1},{1,0},{2,3},{3,2},{4,5},{5,4},{6,7},{7,6},{8,9},{9,8},{10,11... | collective-permute-start | bytes 786440 | tf_op jit(solution)/shard_map/ppermute | solution.py:367
  14.1 1.3 %multiply_cosine_fusion = (f32[1024,16]{0,1:T(8,128)S(1)}, f32[1024,16]{0,1:T(8,128)S(1)}, f32[1024,16]{0,1:T(8,128)S(1)}, f32[1024,16]{0,1:T(8,128)S(1)}) fusion(f32[1024,16]{0,1:T(8,128)} %param.9, f32[]{:T(128)S(6)} %add.18), kind=kLoop, calls=%fused_computation.11 | loop fusion | flops 81920 | bytes 327684 | tf_op jit(solution)/shard_map/cos | solution.py:232
  15.7 0.8 %copy.23 = f32[1,2,32,128]{3,2,1,0:T(8,128)S(1)} copy(f32[1,2,32,128]{3,1,2,0:T(2,128)} %bitcast.53) | data formatting | bytes 65536
  16.4 0.7 pad_maximum_fusion.1.turn
  17.1 0.7 pad_maximum_fusion.base
  17.7 0.0 collective-permute-done.far_side
  17.7 0.0 collective-permute-done.1.near_side
  17.7 4.2 %front.1 = bf16[8,256,128]{2,1,0:T(8,128)(2,1)} custom-call(s32[1]{0:T(128)} %bitcast.1.place, f32[1]{0:T(128)} %bitcast.2.keep, bf16[2,8,64,128]{3,2,1,0:T(8,128)(2,1)S(1)} %collective-permute-done.far_side, bf16[2,16,64,128]{3,2,1,0:T(8,128)(2,1)S(1)} %bitcast.48, bf16[2,8,64,128]{3,2,1,0:T(8,128)(2,1)S(1)} %collective-permute-done.1.near_side, ...), custom_call_target="tpu_custom_call" | custom-call | flops 400000000 | bytes 3000000 | tf_op jit(solution)/shard_map/front/pallas_call | solution.py:181
  22.0 12.2 %all-to-all-start = ((bf16[256,8,128]{2,1,0:T(8,128)(2,1)}), bf16[256,8,128]{2,1,0:T(8,128)(2,1)S(1)}, u32[]{:S(2)}, u32[]{:S(2)}) async-start(bf16[256,8,128]{2,1,0:T(8,128)(2,1)} %bitcast.12), calls=%async_computation | async-start | bytes 1048576 | tf_op jit(solution)/shard_map/all_to_all | solution.py:375
  34.2 6.3 %weights.1.w_far = bf16[16,256,1024]{2,1,0:T(8,128)(2,1)} custom-call(f32[2,16,1024]{2,1,0:T(8,128)} %pad_maximum_fusion.base, f32[2,16,1024]{2,1,0:T(8,128)} %pad_maximum_fusion.1.turn), custom_call_target="tpu_custom_call" | custom-call | flops 20000000 | bytes 9000000 | tf_op jit(solution)/shard_map/weights/pallas_call | solution.py:240
  40.5 14.7 %all-to-all-done = bf16[256,8,128]{2,1,0:T(8,128)(2,1)S(1)} async-done(((bf16[256,8,128]{2,1,0:T(8,128)(2,1)}), bf16[256,8,128]{2,1,0:T(8,128)(2,1)S(1)}, u32[]{:S(2)}, u32[]{:S(2)}) %all-to-all-start) | async-done | bytes 524320 | tf_op jit(solution)/shard_map/all_to_all | solution.py:375
  55.2 14.7 %beams.1 = bf16[32,1,128,1024]{3,2,1,0:T(8,128)(2,1)} custom-call(s32[1]{0:T(128)} %bitcast.lag, bf16[2048,128]{1,0:T(8,128)(2,1)S(1)} %bitcast.49, bf16[16,256,1024]{2,1,0:T(8,128)(2,1)} %weights.1.w_far), custom_call_target="tpu_custom_call" | custom-call | flops 8999999488 | bytes 17000000 | tf_op jit(solution)/shard_map/beams/pallas_call | solution.py:330
  (8 shorter events, 0.3 us)
Async XLA Ops:
  1.2 16.6 %collective-permute-start = (bf16[2,8,64,128]{3,2,1,0:T(8,128)(2,1)S(1)}, bf16[2,8,64,128]{3,2,1,0:T(8,128)(2,1)S(1)}, u32[]{:S(2)}, u32[]{:S(2)}) collective-permute-start(bf16[2,8,64,128]{3,2,1,0:T(8,128)(2,1)S(1)} %bitcast.52), channel_id=1, source_target_pairs={{0,31},{2,1},{4,3},{6,5},{8,7},{10,9},{12,11},{14,13},{16,15},{18,... | collective-permute-start | bytes 786440 | tf_op jit(solution)/shard_map/ppermute | solution.py:366
  6.9 10.8 %collective-permute-start.1 = (bf16[2,8,64,128]{3,2,1,0:T(8,128)(2,1)S(1)}, bf16[2,8,64,128]{3,2,1,0:T(8,128)(2,1)S(1)}, u32[]{:S(2)}, u32[]{:S(2)}) collective-permute-start(bf16[2,8,64,128]{3,2,1,0:T(8,128)(2,1)S(1)} %dynamic-slice_bitcast_fusion), channel_id=1, source_target_pairs={{0,1},{1,0},{2,3},{3,2},{4,5},{5,4},{6,7},{7,6},{8,9},{9,8},{10,11... | collective-permute-start | bytes 786440 | tf_op jit(solution)/shard_map/ppermute | solution.py:367
  22.0 33.2 %all-to-all-start = ((bf16[256,8,128]{2,1,0:T(8,128)(2,1)}), bf16[256,8,128]{2,1,0:T(8,128)(2,1)S(1)}, u32[]{:S(2)}, u32[]{:S(2)}) async-start(bf16[256,8,128]{2,1,0:T(8,128)(2,1)} %bitcast.12), calls=%async_computation | async-start | bytes 1048576 | tf_op jit(solution)/shard_map/all_to_all | solution.py:375

commit v6 on v5

--- a/solution.py
+++ b/solution.py
@@ -71,9 +71,9 @@
     return lanes[0] + lanes[1] if len(lanes) > 1 else lanes[0]
 
 
-def front_kernel(
-    place, keep, far_side, own, near_side, win_far, first_far, twist_far, second_far, gain, out,
-    wide, flt, inter, win, first, twist, second, arrived, ready, left,
+def own_kernel(
+    keep, own, win_far, first_far, twist_far, second_far,
+    partial, win, first, twist, second, wide, arrived,
 ):
     tables = ((win_far, win), (first_far, first), (twist_far, twist), (second_far, second))
     copies = [
@@ -81,41 +81,92 @@
     ]
     for copy in copies:
         copy.start()
+    for i in range(2):
+        wide[i] = own[i].astype(F32)
+    for copy in copies:
+        copy.wait()
+    keep_old = keep[0]
+
+    def filter_step(step, carry):
+        i = step // 8
+        rows = pl.ds(pl.multiple_of((step % 8) * 8, 8), 8)
+        taps = [win[p, rows, :] for p in range(TAPS)]
+        xs = [wide[i, t, rows, :] for t in range(16)]
+        for t in range(16):
+            total = summed([taps[p] * xs[t + p - 7] for p in range(TAPS) if 7 <= t + p < 23])
+            partial[i, t, rows, :] = total * keep_old if t >= 8 else total
+        return carry
+
+    lax.fori_loop(0, 16, filter_step, 0)
+
+
+def far(table):
+    return pltpu.with_memory_space_constraint(jnp.asarray(table), pltpu.HBM)
+
+
+def own_part(keep, own):
+    args = (
+        keep,
+        own,
+        far(window_table()),
+        far(first_table()),
+        far(twist_table()),
+        far(second_table()),
+    )
+    return pl.pallas_call(
+        own_kernel,
+        in_specs=[
+            pl.BlockSpec(memory_space=pltpu.SMEM),
+            pl.BlockSpec(memory_space=pltpu.VMEM),
+        ]
+        + [pl.BlockSpec(memory_space=pltpu.HBM)] * 4,
+        out_shape=(
+            jax.ShapeDtypeStruct((2, 16, INNER, LANES), F32),
+            jax.ShapeDtypeStruct((TAPS, INNER, LANES), F32),
+            jax.ShapeDtypeStruct((128, 192), BF16),
+            jax.ShapeDtypeStruct((2, INNER, LANES), F32),
+            jax.ShapeDtypeStruct((256, LANES), BF16),
+        ),
+        scratch_shapes=[
+            pltpu.VMEM((2, 16, INNER, LANES), F32),
+            pltpu.SemaphoreType.DMA((4,)),
+        ],
+        compiler_params=pltpu.CompilerParams(vmem_limit_bytes=24 << 20),
+        cost_estimate=pl.CostEstimate(flops=8_000_000, bytes_accessed=3_000_000, transcendentals=0),
+        name="own_part",
+    )(*args)
+
+
+def front_kernel(
+    place, far_side, near_side, partial, win, first, twist, second, gain, out,
+    wide, flt, inter, ready, left,
+):
     sends = [
         pltpu.make_async_copy(ready.at[g], out.at[(g + 4) % 8], left.at[g]) for g in range(8)
     ]
-    for i in range(2):
-        wide[i, 7:23] = own[i].astype(F32)
 
     @pl.when(place[0] == 0)
     def _():
         for i in range(2):
             wide[i, 0:7] = far_side[i, 1:8].astype(F32)
-            wide[i, 23:31] = near_side[i].astype(F32)
+            wide[i, 7:15] = near_side[i].astype(F32)
 
     @pl.when(place[0] != 0)
     def _():
         for i in range(2):
             wide[i, 0:7] = near_side[i, 1:8].astype(F32)
-            wide[i, 23:31] = far_side[i].astype(F32)
-
-    keep_old = keep[0]
-    for copy in copies:
-        copy.wait()
+            wide[i, 7:15] = far_side[i].astype(F32)
 
     def filter_step(step, carry):
         i = step // 8
         rows = pl.ds(pl.multiple_of((step % 8) * 8, 8), 8)
         taps = [win[p, rows, :] for p in range(TAPS)]
-        xs = [wide[i, t, rows, :] for t in range(31)]
+        xs = [wide[i, t, rows, :] for t in range(15)]
         for t in range(16):
-            terms = [taps[p] * xs[t + p] for p in range(TAPS)]
-            cut = 23 - t
-            if cut >= TAPS:
-                total = summed(terms)
-            else:
-                total = summed(terms[:cut]) * keep_old + summed(terms[cut:])
-            flt[i, t, rows, :] = total
+            total = partial[i, t, rows, :]
+            terms = [taps[p] * xs[t + p] for p in range(TAPS) if t + p < 7]
+            terms += [taps[p] * xs[t + p - 16] for p in range(TAPS) if t + p >= 23]
+            flt[i, t, rows, :] = total + summed(terms) if terms else total
         return carry
 
     lax.fori_loop(0, 16, filter_step, 0)
@@ -161,40 +212,18 @@
         send.wait()
 
 
-def far(table):
-    return pltpu.with_memory_space_constraint(jnp.asarray(table), pltpu.HBM)
-
-
-def front(place, keep, far_side, own, near_side, gain):
-    args = (
-        place,
-        keep,
-        far_side,
-        own,
-        near_side,
-        far(window_table()),
-        far(first_table()),
-        far(twist_table()),
-        far(second_table()),
-        gain,
-    )
+def front(place, far_side, near_side, own, gain):
+    args = (place, far_side, near_side, *own, gain)
     return pl.pallas_call(
         front_kernel,
-        in_specs=[pl.BlockSpec(memory_space=pltpu.SMEM)] * 2
-        + [pl.BlockSpec(memory_space=pltpu.VMEM)] * 3
-        + [pl.BlockSpec(memory_space=pltpu.HBM)] * 4
-        + [pl.BlockSpec(memory_space=pltpu.VMEM)],
+        in_specs=[pl.BlockSpec(memory_space=pltpu.SMEM)]
+        + [pl.BlockSpec(memory_space=pltpu.VMEM)] * 8,
         out_specs=pl.BlockSpec(memory_space=pltpu.HBM),
         out_shape=jax.ShapeDtypeStruct((8, 256, LANES), BF16),
         scratch_shapes=[
-            pltpu.VMEM((2, 31, INNER, LANES), F32),
+            pltpu.VMEM((2, 15, INNER, LANES), F32),
             pltpu.VMEM((2, 16, INNER, LANES), F32),
             pltpu.VMEM((8, 264, LANES), F32),
-            pltpu.VMEM((TAPS, INNER, LANES), F32),
-            pltpu.VMEM((128, 192), BF16),
-            pltpu.VMEM((2, INNER, LANES), F32),
-            pltpu.VMEM((256, LANES), BF16),
-            pltpu.SemaphoreType.DMA((4,)),
             pltpu.VMEM((8, 256, LANES), BF16),
             pltpu.SemaphoreType.DMA((8,)),
         ],
@@ -367,11 +396,12 @@
     near_side = lax.ppermute(inner, "shard", [(at, at ^ 1) for at in range(count)])
     keep = jnp.where(shard == count - 1, 0.0, 1.0).astype(F32).reshape(1)
     chan_here = CHANNELS // count
+    own = own_part(keep, frames)
     base, turn, gain = lax.optimization_barrier(
         (*angles(delays, shard * chan_here), eq_gain.reshape(2, 32, LANES))
     )
     place = place.astype(jnp.int32).reshape(1)
-    messages = front(place, keep, far_side, frames, near_side, gain)
+    messages = front(place, far_side, near_side, own, gain)
     got = lax.all_to_all(
         messages.reshape(256, 8, LANES), ("grp", "shard"), split_axis=0, concat_axis=0, tiled=True
     )

time: 70.2 us -> 68.4 us (0.974)
  starting transfers between devices: 23.9 us -> 21.7 us
    all_to_all x1, starting transfers between devices: 12.2 us -> 10 us  [per_device(): lax.all_to_all(messages.reshape(256, 8, LANES), ('grp', 'shard'), split_a...]
    pallas_call x0 -> x1, Pallas kernels: none -> 2.13 us  [own_part(): pl.pallas_call(own_kernel, in_specs=[pl.BlockSpec(memory_space=pltpu.SMEM...]
    pallas_call x1, Pallas kernels: 4.25 us -> 2.43 us  [front(): pl.pallas_call(front_kernel, in_specs=[pl.BlockSpec(memory_space=pltpu.SM...]
  transfers between devices with their start and end apart: 3 -> 3, of which waited for: 1 -> 1; matrix products, arithmetic and copies ran while one was open for 7% -> 7% of each run, Pallas kernels for 9% -> 12%
where the time goes in v6:
time: 68.4 us; the launch traced here: 68 us
  Pallas kernels  25.5 us (37%)
  starting transfers between devices  21.7 us (32%)
  waiting for transfers between devices  14.7 us (21%)
  local copies, waits for them, and re-layouts  3.32 us (5%)
  other arithmetic  2.61 us (4%)
    all_to_all x1, waiting for transfers between devices, per_device(): lax.all_to_all(messages.reshape(256, 8, LANES), ('grp', 'shard'), split_a...  14.7 us
    pallas_call x1, Pallas kernels, beams_of(): pl.pallas_call(beam_kernel, grid=(chan_here // 32,), in_specs=[pl.BlockSp...  14.7 us
    all_to_all x1, starting transfers between devices, per_device(): lax.all_to_all(messages.reshape(256, 8, LANES), ('grp', 'shard'), split_a...  10 us
    ppermute x1, starting transfers between devices, per_device(): lax.ppermute(inner, 'shard', [(at, at ^ 1) for at in range(count)])  7.11 us
    pallas_call x1, Pallas kernels, weights(): pl.pallas_call(weight_kernel, grid=(groups // 2,), in_specs=[whole, whole...  6.27 us
    ppermute x1, starting transfers between devices, per_device(): lax.ppermute(outer, 'shard', swaps + [(at, at + 1) for at in range(1, cou...  4.59 us
    unnamed x4, local copies, waits for them, and re-layouts  3.04 us
    pallas_call x1, Pallas kernels, front(): pl.pallas_call(front_kernel, in_specs=[pl.BlockSpec(memory_space=pltpu.SM...  2.43 us
  transfers between devices with their start and end apart: 3, of which 1 were waited for; matrix products, arithmetic and copies ran while one was open for 7% of the time, Pallas kernels for 12%

profile of v6, /device:TPU:1, one launch (start us, length us, event | category | flops | bytes accessed | tf_op | source)
XLA Modules:
  0.0 68.0 jit_solution(13244623258965601781)
XLA Ops:
  0.0 1.1 %dynamic-slice_bitcast_fusion.1 = bf16[1,2,512,128]{3,1,2,0:T(2,128)(2,1)S(1)} fusion(bf16[2,131072]{1,0:T(2,128)(2,1)} %param.7, s32[]{:T(128)S(6)} %select_n.24), kind=kLoop, calls=%fused_computation.1 | loop fusion | bytes 524292
  1.2 4.6 %collective-permute-start = (bf16[2,8,64,128]{3,2,1,0:T(8,128)(2,1)S(1)}, bf16[2,8,64,128]{3,2,1,0:T(8,128)(2,1)S(1)}, u32[]{:S(2)}, u32[]{:S(2)}) collective-permute-start(bf16[2,8,64,128]{3,2,1,0:T(8,128)(2,1)S(1)} %bitcast.52), channel_id=1, source_target_pairs={{0,31},{2,1},{4,3},{6,5},{8,7},{10,9},{12,11},{14,13},{16,15},{18,... | collective-permute-start | bytes 786440 | tf_op jit(solution)/shard_map/ppermute | solution.py:395
  5.8 1.1 %copy.15 = bf16[1,2,1024,128]{3,2,1,0:T(8,128)(2,1)S(1)} copy(bf16[1,2,1024,128]{3,1,2,0:T(2,128)(2,1)} %bitcast.51) | data formatting | bytes 1048576
  6.9 7.1 %collective-permute-start.1 = (bf16[2,8,64,128]{3,2,1,0:T(8,128)(2,1)S(1)}, bf16[2,8,64,128]{3,2,1,0:T(8,128)(2,1)S(1)}, u32[]{:S(2)}, u32[]{:S(2)}) collective-permute-start(bf16[2,8,64,128]{3,2,1,0:T(8,128)(2,1)S(1)} %dynamic-slice_bitcast_fusion), channel_id=1, source_target_pairs={{0,1},{1,0},{2,3},{3,2},{4,5},{5,4},{6,7},{7,6},{8,9},{9,8},{10,11... | collective-permute-start | bytes 786440 | tf_op jit(solution)/shard_map/ppermute | solution.py:396
  14.1 1.3 %multiply_cosine_fusion = (f32[1024,16]{0,1:T(8,128)S(1)}, f32[1024,16]{0,1:T(8,128)S(1)}, f32[1024,16]{0,1:T(8,128)S(1)}, f32[1024,16]{0,1:T(8,128)S(1)}) fusion(f32[1024,16]{0,1:T(8,128)} %param.9, f32[]{:T(128)S(6)} %add.18), kind=kLoop, calls=%fused_computation.11 | loop fusion | flops 81920 | bytes 327684 | tf_op jit(solution)/shard_map/cos | solution.py:261
  15.7 0.8 %copy.23 = f32[1,2,32,128]{3,2,1,0:T(8,128)S(1)} copy(f32[1,2,32,128]{3,1,2,0:T(2,128)} %bitcast.53) | data formatting | bytes 65536
  16.4 0.7 pad_maximum_fusion.1.turn
  17.1 0.6 pad_maximum_fusion.base
  17.7 2.1 %own_part.1 = (f32[2,16,64,128]{3,2,1,0:T(8,128)S(1)}, f32[16,64,128]{2,1,0:T(8,128)S(1)}, bf16[128,192]{1,0:T(8,128)(2,1)S(1)}, f32[2,64,128]{2,1,0:T(8,128)S(1)}, bf16[256,128]{1,0:T(8,128)(2,1)S(1)}) custom-call(f32[1]{0:T(128)} %bitcast.3.keep, bf16[2,16,64,128]{3,2,1,0:T(8,128)(2,1)S(1)} %bitcast.48, f32[16,64,128]{2,1,0:T(8,128)} %constant.59.clone.win_far, ...), custom_call_target="tpu_custom_call" | custom-call | flops 8000000 | bytes 3000000 | tf_op jit(solution)/shard_map/own_part/pallas_call | solution.py:116
  19.9 0.0 collective-permute-done.far_side
  19.9 0.0 collective-permute-done.1.near_side
  19.9 2.4 %front.1 = bf16[8,256,128]{2,1,0:T(8,128)(2,1)} custom-call(s32[1]{0:T(128)} %bitcast.1.place, bf16[2,8,64,128]{3,2,1,0:T(8,128)(2,1)S(1)} %collective-permute-done.far_side, bf16[2,8,64,128]{3,2,1,0:T(8,128)(2,1)S(1)} %collective-permute-done.1.near_side, f32[2,16,64,128]{3,2,1,0:T(8,128)S(1)} %get-tuple-element.13.partial, ...), custom_call_target="tpu_custom_call" | custom-call | flops 400000000 | bytes 3000000 | tf_op jit(solution)/shard_map/front/pallas_call | solution.py:217
  22.3 10.0 %all-to-all-start = ((bf16[256,8,128]{2,1,0:T(8,128)(2,1)}), bf16[256,8,128]{2,1,0:T(8,128)(2,1)S(1)}, u32[]{:S(2)}, u32[]{:S(2)}) async-start(bf16[256,8,128]{2,1,0:T(8,128)(2,1)} %bitcast.12), calls=%async_computation | async-start | bytes 1048576 | tf_op jit(solution)/shard_map/all_to_all | solution.py:405
  32.4 6.3 %weights.1.w_far = bf16[16,256,1024]{2,1,0:T(8,128)(2,1)} custom-call(f32[2,16,1024]{2,1,0:T(8,128)} %pad_maximum_fusion.base, f32[2,16,1024]{2,1,0:T(8,128)} %pad_maximum_fusion.1.turn), custom_call_target="tpu_custom_call" | custom-call | flops 20000000 | bytes 9000000 | tf_op jit(solution)/shard_map/weights/pallas_call | solution.py:269
  38.6 14.7 %all-to-all-done = bf16[256,8,128]{2,1,0:T(8,128)(2,1)S(1)} async-done(((bf16[256,8,128]{2,1,0:T(8,128)(2,1)}), bf16[256,8,128]{2,1,0:T(8,128)(2,1)S(1)}, u32[]{:S(2)}, u32[]{:S(2)}) %all-to-all-start) | async-done | bytes 524320 | tf_op jit(solution)/shard_map/all_to_all | solution.py:405
  53.4 14.7 %beams.1 = bf16[32,1,128,1024]{3,2,1,0:T(8,128)(2,1)} custom-call(s32[1]{0:T(128)} %bitcast.lag, bf16[2048,128]{1,0:T(8,128)(2,1)S(1)} %bitcast.49, bf16[16,256,1024]{2,1,0:T(8,128)(2,1)} %weights.1.w_far), custom_call_target="tpu_custom_call" | custom-call | flops 8999999488 | bytes 17000000 | tf_op jit(solution)/shard_map/beams/pallas_call | solution.py:359
  (8 shorter events, 0.3 us)
Async XLA Ops:
  1.2 18.7 %collective-permute-start = (bf16[2,8,64,128]{3,2,1,0:T(8,128)(2,1)S(1)}, bf16[2,8,64,128]{3,2,1,0:T(8,128)(2,1)S(1)}, u32[]{:S(2)}, u32[]{:S(2)}) collective-permute-start(bf16[2,8,64,128]{3,2,1,0:T(8,128)(2,1)S(1)} %bitcast.52), channel_id=1, source_target_pairs={{0,31},{2,1},{4,3},{6,5},{8,7},{10,9},{12,11},{14,13},{16,15},{18,... | collective-permute-start | bytes 786440 | tf_op jit(solution)/shard_map/ppermute | solution.py:395
  6.9 12.9 %collective-permute-start.1 = (bf16[2,8,64,128]{3,2,1,0:T(8,128)(2,1)S(1)}, bf16[2,8,64,128]{3,2,1,0:T(8,128)(2,1)S(1)}, u32[]{:S(2)}, u32[]{:S(2)}) collective-permute-start(bf16[2,8,64,128]{3,2,1,0:T(8,128)(2,1)S(1)} %dynamic-slice_bitcast_fusion), channel_id=1, source_target_pairs={{0,1},{1,0},{2,3},{3,2},{4,5},{5,4},{6,7},{7,6},{8,9},{9,8},{10,11... | collective-permute-start | bytes 786440 | tf_op jit(solution)/shard_map/ppermute | solution.py:396
  22.3 31.0 %all-to-all-start = ((bf16[256,8,128]{2,1,0:T(8,128)(2,1)}), bf16[256,8,128]{2,1,0:T(8,128)(2,1)S(1)}, u32[]{:S(2)}, u32[]{:S(2)}) async-start(bf16[256,8,128]{2,1,0:T(8,128)(2,1)} %bitcast.12), calls=%async_computation | async-start | bytes 1048576 | tf_op jit(solution)/shard_map/all_to_all | solution.py:405

commit v7 on v6

--- a/solution.py
+++ b/solution.py
@@ -279,13 +279,13 @@
     )(base, turn)
 
 
-def beam_kernel(lag, spec, w_far, out, held, arrived, wide, flat, left, right, l2, l3):
+def beam_kernel(lag, spec, w_far, out, held, arrived, wide, flat, *sides):
     step = pl.program_id(0)
     slot = lax.rem(step, 2)
     w = held.at[slot]
 
     def fetch(at, into):
-        blocks = w_far.at[pl.ds(at * 4, 4)]
+        blocks = w_far.at[pl.ds(at * 8, 8)]
         return pltpu.make_async_copy(blocks, held.at[into], arrived.at[into])
 
     lane = lax.broadcasted_iota(jnp.int32, (8, LANES), 1) // 32
@@ -346,36 +346,32 @@
             both = jnp.concatenate(powers, axis=1) * (1.0 / INPUTS)
             out[:, 0, pair * 16 : pair * 16 + 16, cols] = both.astype(BF16)
 
-    spread_out(step * 32, left)
-    spread_out(step * 32 + 8, right)
-    form(0, (left, right))
-    spread_out(step * 32 + 16, l2)
-    spread_out(step * 32 + 24, l3)
-    form(1, (l2, l3))
+    for pair in range(4):
+        refs = sides[2 * pair : 2 * pair + 2]
+        for group in range(2):
+            spread_out(step * 64 + pair * 16 + group * 8, refs[group])
+        form(pair, refs)
 
 
 def beams_of(lag, spec, w, chan_here):
     count = w.shape[2]
     return pl.pallas_call(
         beam_kernel,
-        grid=(chan_here // 32,),
+        grid=(chan_here // 64,),
         in_specs=[
             pl.BlockSpec(memory_space=pltpu.SMEM),
             pl.BlockSpec(memory_space=pltpu.VMEM),
             pl.BlockSpec(memory_space=pltpu.HBM),
         ],
-        out_specs=pl.BlockSpec((32, 1, 32, count), lambda k: (0, 0, k, 0)),
+        out_specs=pl.BlockSpec((32, 1, 64, count), lambda k: (0, 0, k, 0)),
         out_shape=jax.ShapeDtypeStruct((32, 1, chan_here, count), BF16),
         scratch_shapes=[
-            pltpu.VMEM((2, 4, 256, count), BF16),
+            pltpu.VMEM((2, 8, 256, count), BF16),
             pltpu.SemaphoreType.DMA((2,)),
             pltpu.VMEM((2304, LANES), F32),
             pltpu.VMEM((2, 16, LANES, LANES), F32),
-            pltpu.VMEM((1024, 256), BF16),
-            pltpu.VMEM((1024, 256), BF16),
-            pltpu.VMEM((1024, 256), BF16),
-            pltpu.VMEM((1024, 256), BF16),
-        ],
+        ]
+        + [pltpu.VMEM((1024, 256), BF16)] * 8,
         compiler_params=pltpu.CompilerParams(vmem_limit_bytes=40 << 20),
         cost_estimate=pl.CostEstimate(flops=9_000_000_000, bytes_accessed=17_000_000, transcendentals=0),
         name="beams",

time: 68.4 us -> 68.5 us (level)
  no operation moved by 1% of the time
where the time goes in v7:
time: 68.5 us; the launch traced here: 68.2 us
  Pallas kernels  25.6 us (37%)
  starting transfers between devices  21.7 us (32%)
  waiting for transfers between devices  14.7 us (21%)
  local copies, waits for them, and re-layouts  3.32 us (5%)
  other arithmetic  2.61 us (4%)
    pallas_call x1, Pallas kernels, beams_of(): pl.pallas_call(beam_kernel, grid=(chan_here // 64,), in_specs=[pl.BlockSp...  14.8 us
    all_to_all x1, waiting for transfers between devices, per_device(): lax.all_to_all(messages.reshape(256, 8, LANES), ('grp', 'shard'), split_a...  14.7 us
    all_to_all x1, starting transfers between devices, per_device(): lax.all_to_all(messages.reshape(256, 8, LANES), ('grp', 'shard'), split_a...  10 us
    ppermute x1, starting transfers between devices, per_device(): lax.ppermute(inner, 'shard', [(at, at ^ 1) for at in range(count)])  7.11 us
    pallas_call x1, Pallas kernels, weights(): pl.pallas_call(weight_kernel, grid=(groups // 2,), in_specs=[whole, whole...  6.27 us
    ppermute x1, starting transfers between devices, per_device(): lax.ppermute(outer, 'shard', swaps + [(at, at + 1) for at in range(1, cou...  4.59 us
    unnamed x4, local copies, waits for them, and re-layouts  3.04 us
    pallas_call x1, Pallas kernels, front(): pl.pallas_call(front_kernel, in_specs=[pl.BlockSpec(memory_space=pltpu.SM...  2.43 us
  transfers between devices with their start and end apart: 3, of which 1 were waited for; matrix products, arithmetic and copies ran while one was open for 7% of the time, Pallas kernels for 12%

profile of v7, /device:TPU:1, one launch (start us, length us, event | category | flops | bytes accessed | tf_op | source)
XLA Modules:
  0.0 68.2 jit_solution(18342360095287844903)
XLA Ops:
  0.0 1.1 %dynamic-slice_bitcast_fusion.1 = bf16[1,2,512,128]{3,1,2,0:T(2,128)(2,1)S(1)} fusion(bf16[2,131072]{1,0:T(2,128)(2,1)} %param.7, s32[]{:T(128)S(6)} %select_n.24), kind=kLoop, calls=%fused_computation.1 | loop fusion | bytes 524292
  1.2 4.6 %collective-permute-start = (bf16[2,8,64,128]{3,2,1,0:T(8,128)(2,1)S(1)}, bf16[2,8,64,128]{3,2,1,0:T(8,128)(2,1)S(1)}, u32[]{:S(2)}, u32[]{:S(2)}) collective-permute-start(bf16[2,8,64,128]{3,2,1,0:T(8,128)(2,1)S(1)} %bitcast.52), channel_id=1, source_target_pairs={{0,31},{2,1},{4,3},{6,5},{8,7},{10,9},{12,11},{14,13},{16,15},{18,... | collective-permute-start | bytes 786440 | tf_op jit(solution)/shard_map/ppermute | solution.py:391
  5.8 1.1 %copy.15 = bf16[1,2,1024,128]{3,2,1,0:T(8,128)(2,1)S(1)} copy(bf16[1,2,1024,128]{3,1,2,0:T(2,128)(2,1)} %bitcast.51) | data formatting | bytes 1048576
  6.9 7.1 %collective-permute-start.1 = (bf16[2,8,64,128]{3,2,1,0:T(8,128)(2,1)S(1)}, bf16[2,8,64,128]{3,2,1,0:T(8,128)(2,1)S(1)}, u32[]{:S(2)}, u32[]{:S(2)}) collective-permute-start(bf16[2,8,64,128]{3,2,1,0:T(8,128)(2,1)S(1)} %dynamic-slice_bitcast_fusion), channel_id=1, source_target_pairs={{0,1},{1,0},{2,3},{3,2},{4,5},{5,4},{6,7},{7,6},{8,9},{9,8},{10,11... | collective-permute-start | bytes 786440 | tf_op jit(solution)/shard_map/ppermute | solution.py:392
  14.1 1.3 %multiply_cosine_fusion = (f32[1024,16]{0,1:T(8,128)S(1)}, f32[1024,16]{0,1:T(8,128)S(1)}, f32[1024,16]{0,1:T(8,128)S(1)}, f32[1024,16]{0,1:T(8,128)S(1)}) fusion(f32[1024,16]{0,1:T(8,128)} %param.9, f32[]{:T(128)S(6)} %add.18), kind=kLoop, calls=%fused_computation.11 | loop fusion | flops 81920 | bytes 327684 | tf_op jit(solution)/shard_map/cos | solution.py:261
  15.7 0.8 %copy.23 = f32[1,2,32,128]{3,2,1,0:T(8,128)S(1)} copy(f32[1,2,32,128]{3,1,2,0:T(2,128)} %bitcast.53) | data formatting | bytes 65536
  16.4 0.7 pad_maximum_fusion.1.turn
  17.1 0.6 pad_maximum_fusion.base
  17.7 2.1 %own_part.1 = (f32[2,16,64,128]{3,2,1,0:T(8,128)S(1)}, f32[16,64,128]{2,1,0:T(8,128)S(1)}, bf16[128,192]{1,0:T(8,128)(2,1)S(1)}, f32[2,64,128]{2,1,0:T(8,128)S(1)}, bf16[256,128]{1,0:T(8,128)(2,1)S(1)}) custom-call(f32[1]{0:T(128)} %bitcast.3.keep, bf16[2,16,64,128]{3,2,1,0:T(8,128)(2,1)S(1)} %bitcast.48, f32[16,64,128]{2,1,0:T(8,128)} %constant.59.clone.win_far, ...), custom_call_target="tpu_custom_call" | custom-call | flops 8000000 | bytes 3000000 | tf_op jit(solution)/shard_map/own_part/pallas_call | solution.py:116
  19.9 0.0 collective-permute-done.far_side
  19.9 0.0 collective-permute-done.1.near_side
  19.9 2.4 %front.1 = bf16[8,256,128]{2,1,0:T(8,128)(2,1)} custom-call(s32[1]{0:T(128)} %bitcast.1.place, bf16[2,8,64,128]{3,2,1,0:T(8,128)(2,1)S(1)} %collective-permute-done.far_side, bf16[2,8,64,128]{3,2,1,0:T(8,128)(2,1)S(1)} %collective-permute-done.1.near_side, f32[2,16,64,128]{3,2,1,0:T(8,128)S(1)} %get-tuple-element.13.partial, ...), custom_call_target="tpu_custom_call" | custom-call | flops 400000000 | bytes 3000000 | tf_op jit(solution)/shard_map/front/pallas_call | solution.py:217
  22.3 10.0 %all-to-all-start = ((bf16[256,8,128]{2,1,0:T(8,128)(2,1)}), bf16[256,8,128]{2,1,0:T(8,128)(2,1)S(1)}, u32[]{:S(2)}, u32[]{:S(2)}) async-start(bf16[256,8,128]{2,1,0:T(8,128)(2,1)} %bitcast.12), calls=%async_computation | async-start | bytes 1048576 | tf_op jit(solution)/shard_map/all_to_all | solution.py:401
  32.4 6.3 %weights.1.w_far = bf16[16,256,1024]{2,1,0:T(8,128)(2,1)} custom-call(f32[2,16,1024]{2,1,0:T(8,128)} %pad_maximum_fusion.base, f32[2,16,1024]{2,1,0:T(8,128)} %pad_maximum_fusion.1.turn), custom_call_target="tpu_custom_call" | custom-call | flops 20000000 | bytes 9000000 | tf_op jit(solution)/shard_map/weights/pallas_call | solution.py:269
  38.6 14.7 %all-to-all-done = bf16[256,8,128]{2,1,0:T(8,128)(2,1)S(1)} async-done(((bf16[256,8,128]{2,1,0:T(8,128)(2,1)}), bf16[256,8,128]{2,1,0:T(8,128)(2,1)S(1)}, u32[]{:S(2)}, u32[]{:S(2)}) %all-to-all-start) | async-done | bytes 524320 | tf_op jit(solution)/shard_map/all_to_all | solution.py:401
  53.4 14.8 %beams.1 = bf16[32,1,128,1024]{3,2,1,0:T(8,128)(2,1)} custom-call(s32[1]{0:T(128)} %bitcast.lag, bf16[2048,128]{1,0:T(8,128)(2,1)S(1)} %bitcast.49, bf16[16,256,1024]{2,1,0:T(8,128)(2,1)} %weights.1.w_far), custom_call_target="tpu_custom_call" | custom-call | flops 8999999488 | bytes 17000000 | tf_op jit(solution)/shard_map/beams/pallas_call | solution.py:358
  (8 shorter events, 0.3 us)
Async XLA Ops:
  1.2 18.7 %collective-permute-start = (bf16[2,8,64,128]{3,2,1,0:T(8,128)(2,1)S(1)}, bf16[2,8,64,128]{3,2,1,0:T(8,128)(2,1)S(1)}, u32[]{:S(2)}, u32[]{:S(2)}) collective-permute-start(bf16[2,8,64,128]{3,2,1,0:T(8,128)(2,1)S(1)} %bitcast.52), channel_id=1, source_target_pairs={{0,31},{2,1},{4,3},{6,5},{8,7},{10,9},{12,11},{14,13},{16,15},{18,... | collective-permute-start | bytes 786440 | tf_op jit(solution)/shard_map/ppermute | solution.py:391
  6.9 12.9 %collective-permute-start.1 = (bf16[2,8,64,128]{3,2,1,0:T(8,128)(2,1)S(1)}, bf16[2,8,64,128]{3,2,1,0:T(8,128)(2,1)S(1)}, u32[]{:S(2)}, u32[]{:S(2)}) collective-permute-start(bf16[2,8,64,128]{3,2,1,0:T(8,128)(2,1)S(1)} %dynamic-slice_bitcast_fusion), channel_id=1, source_target_pairs={{0,1},{1,0},{2,3},{3,2},{4,5},{5,4},{6,7},{7,6},{8,9},{9,8},{10,11... | collective-permute-start | bytes 786440 | tf_op jit(solution)/shard_map/ppermute | solution.py:392
  22.3 31.0 %all-to-all-start = ((bf16[256,8,128]{2,1,0:T(8,128)(2,1)}), bf16[256,8,128]{2,1,0:T(8,128)(2,1)S(1)}, u32[]{:S(2)}, u32[]{:S(2)}) async-start(bf16[256,8,128]{2,1,0:T(8,128)(2,1)} %bitcast.12), calls=%async_computation | async-start | bytes 1048576 | tf_op jit(solution)/shard_map/all_to_all | solution.py:401

commit v8 on v6

--- a/solution.py
+++ b/solution.py
@@ -169,7 +169,7 @@
             flt[i, t, rows, :] = total + summed(terms) if terms else total
         return carry
 
-    lax.fori_loop(0, 16, filter_step, 0)
+    lax.fori_loop(0, 16, filter_step, 0, unroll=4)
 
     low_lanes = lax.broadcasted_iota(jnp.int32, (64, LANES), 1) < 64
 

time: 68.4 us -> 68.3 us (level)
  no operation moved by 1% of the time
where the time goes in v8:
time: 68.3 us; the launch traced here: 67.9 us
  Pallas kernels  25.4 us (37%)
  starting transfers between devices  21.7 us (32%)
  waiting for transfers between devices  14.7 us (22%)
  local copies, waits for them, and re-layouts  3.32 us (5%)
  other arithmetic  2.61 us (4%)
    all_to_all x1, waiting for transfers between devices, per_device(): lax.all_to_all(messages.reshape(256, 8, LANES), ('grp', 'shard'), split_a...  14.7 us
    pallas_call x1, Pallas kernels, beams_of(): pl.pallas_call(beam_kernel, grid=(chan_here // 32,), in_specs=[pl.BlockSp...  14.7 us
    all_to_all x1, starting transfers between devices, per_device(): lax.all_to_all(messages.reshape(256, 8, LANES), ('grp', 'shard'), split_a...  10 us
    ppermute x1, starting transfers between devices, per_device(): lax.ppermute(inner, 'shard', [(at, at ^ 1) for at in range(count)])  7.11 us
    pallas_call x1, Pallas kernels, weights(): pl.pallas_call(weight_kernel, grid=(groups // 2,), in_specs=[whole, whole...  6.27 us
    ppermute x1, starting transfers between devices, per_device(): lax.ppermute(outer, 'shard', swaps + [(at, at + 1) for at in range(1, cou...  4.59 us
    unnamed x4, local copies, waits for them, and re-layouts  3.04 us
    pallas_call x1, Pallas kernels, front(): pl.pallas_call(front_kernel, in_specs=[pl.BlockSpec(memory_space=pltpu.SM...  2.33 us
  transfers between devices with their start and end apart: 3, of which 1 were waited for; matrix products, arithmetic and copies ran while one was open for 7% of the time, Pallas kernels for 12%

profile of v8, /device:TPU:1, one launch (start us, length us, event | category | flops | bytes accessed | tf_op | source)
XLA Modules:
  0.0 67.9 jit_solution(11555847165226391743)
XLA Ops:
  0.0 1.1 %dynamic-slice_bitcast_fusion.1 = bf16[1,2,512,128]{3,1,2,0:T(2,128)(2,1)S(1)} fusion(bf16[2,131072]{1,0:T(2,128)(2,1)} %param.7, s32[]{:T(128)S(6)} %select_n.24), kind=kLoop, calls=%fused_computation.1 | loop fusion | bytes 524292
  1.2 4.6 %collective-permute-start = (bf16[2,8,64,128]{3,2,1,0:T(8,128)(2,1)S(1)}, bf16[2,8,64,128]{3,2,1,0:T(8,128)(2,1)S(1)}, u32[]{:S(2)}, u32[]{:S(2)}) collective-permute-start(bf16[2,8,64,128]{3,2,1,0:T(8,128)(2,1)S(1)} %bitcast.52), channel_id=1, source_target_pairs={{0,31},{2,1},{4,3},{6,5},{8,7},{10,9},{12,11},{14,13},{16,15},{18,... | collective-permute-start | bytes 786440 | tf_op jit(solution)/shard_map/ppermute | solution.py:395
  5.8 1.1 %copy.15 = bf16[1,2,1024,128]{3,2,1,0:T(8,128)(2,1)S(1)} copy(bf16[1,2,1024,128]{3,1,2,0:T(2,128)(2,1)} %bitcast.51) | data formatting | bytes 1048576
  6.9 7.1 %collective-permute-start.1 = (bf16[2,8,64,128]{3,2,1,0:T(8,128)(2,1)S(1)}, bf16[2,8,64,128]{3,2,1,0:T(8,128)(2,1)S(1)}, u32[]{:S(2)}, u32[]{:S(2)}) collective-permute-start(bf16[2,8,64,128]{3,2,1,0:T(8,128)(2,1)S(1)} %dynamic-slice_bitcast_fusion), channel_id=1, source_target_pairs={{0,1},{1,0},{2,3},{3,2},{4,5},{5,4},{6,7},{7,6},{8,9},{9,8},{10,11... | collective-permute-start | bytes 786440 | tf_op jit(solution)/shard_map/ppermute | solution.py:396
  14.1 1.3 %multiply_cosine_fusion = (f32[1024,16]{0,1:T(8,128)S(1)}, f32[1024,16]{0,1:T(8,128)S(1)}, f32[1024,16]{0,1:T(8,128)S(1)}, f32[1024,16]{0,1:T(8,128)S(1)}) fusion(f32[1024,16]{0,1:T(8,128)} %param.9, f32[]{:T(128)S(6)} %add.18), kind=kLoop, calls=%fused_computation.11 | loop fusion | flops 81920 | bytes 327684 | tf_op jit(solution)/shard_map/cos | solution.py:261
  15.7 0.8 %copy.23 = f32[1,2,32,128]{3,2,1,0:T(8,128)S(1)} copy(f32[1,2,32,128]{3,1,2,0:T(2,128)} %bitcast.53) | data formatting | bytes 65536
  16.4 0.7 pad_maximum_fusion.1.turn
  17.1 0.6 pad_maximum_fusion.base
  17.7 2.1 %own_part.1 = (f32[2,16,64,128]{3,2,1,0:T(8,128)S(1)}, f32[16,64,128]{2,1,0:T(8,128)S(1)}, bf16[128,192]{1,0:T(8,128)(2,1)S(1)}, f32[2,64,128]{2,1,0:T(8,128)S(1)}, bf16[256,128]{1,0:T(8,128)(2,1)S(1)}) custom-call(f32[1]{0:T(128)} %bitcast.3.keep, bf16[2,16,64,128]{3,2,1,0:T(8,128)(2,1)S(1)} %bitcast.48, f32[16,64,128]{2,1,0:T(8,128)} %constant.59.clone.win_far, ...), custom_call_target="tpu_custom_call" | custom-call | flops 8000000 | bytes 3000000 | tf_op jit(solution)/shard_map/own_part/pallas_call | solution.py:116
  19.9 0.0 collective-permute-done.far_side
  19.9 0.0 collective-permute-done.1.near_side
  19.9 2.3 %front.1 = bf16[8,256,128]{2,1,0:T(8,128)(2,1)} custom-call(s32[1]{0:T(128)} %bitcast.1.place, bf16[2,8,64,128]{3,2,1,0:T(8,128)(2,1)S(1)} %collective-permute-done.far_side, bf16[2,8,64,128]{3,2,1,0:T(8,128)(2,1)S(1)} %collective-permute-done.1.near_side, f32[2,16,64,128]{3,2,1,0:T(8,128)S(1)} %get-tuple-element.13.partial, ...), custom_call_target="tpu_custom_call" | custom-call | flops 400000000 | bytes 3000000 | tf_op jit(solution)/shard_map/front/pallas_call | solution.py:217
  22.2 10.0 %all-to-all-start = ((bf16[256,8,128]{2,1,0:T(8,128)(2,1)}), bf16[256,8,128]{2,1,0:T(8,128)(2,1)S(1)}, u32[]{:S(2)}, u32[]{:S(2)}) async-start(bf16[256,8,128]{2,1,0:T(8,128)(2,1)} %bitcast.12), calls=%async_computation | async-start | bytes 1048576 | tf_op jit(solution)/shard_map/all_to_all | solution.py:405
  32.3 6.3 %weights.1.w_far = bf16[16,256,1024]{2,1,0:T(8,128)(2,1)} custom-call(f32[2,16,1024]{2,1,0:T(8,128)} %pad_maximum_fusion.base, f32[2,16,1024]{2,1,0:T(8,128)} %pad_maximum_fusion.1.turn), custom_call_target="tpu_custom_call" | custom-call | flops 20000000 | bytes 9000000 | tf_op jit(solution)/shard_map/weights/pallas_call | solution.py:269
  38.5 14.7 %all-to-all-done = bf16[256,8,128]{2,1,0:T(8,128)(2,1)S(1)} async-done(((bf16[256,8,128]{2,1,0:T(8,128)(2,1)}), bf16[256,8,128]{2,1,0:T(8,128)(2,1)S(1)}, u32[]{:S(2)}, u32[]{:S(2)}) %all-to-all-start) | async-done | bytes 524320 | tf_op jit(solution)/shard_map/all_to_all | solution.py:405
  53.3 14.7 %beams.1 = bf16[32,1,128,1024]{3,2,1,0:T(8,128)(2,1)} custom-call(s32[1]{0:T(128)} %bitcast.lag, bf16[2048,128]{1,0:T(8,128)(2,1)S(1)} %bitcast.49, bf16[16,256,1024]{2,1,0:T(8,128)(2,1)} %weights.1.w_far), custom_call_target="tpu_custom_call" | custom-call | flops 8999999488 | bytes 17000000 | tf_op jit(solution)/shard_map/beams/pallas_call | solution.py:359
  (8 shorter events, 0.3 us)
Async XLA Ops:
  1.2 18.7 %collective-permute-start = (bf16[2,8,64,128]{3,2,1,0:T(8,128)(2,1)S(1)}, bf16[2,8,64,128]{3,2,1,0:T(8,128)(2,1)S(1)}, u32[]{:S(2)}, u32[]{:S(2)}) collective-permute-start(bf16[2,8,64,128]{3,2,1,0:T(8,128)(2,1)S(1)} %bitcast.52), channel_id=1, source_target_pairs={{0,31},{2,1},{4,3},{6,5},{8,7},{10,9},{12,11},{14,13},{16,15},{18,... | collective-permute-start | bytes 786440 | tf_op jit(solution)/shard_map/ppermute | solution.py:395
  6.9 12.9 %collective-permute-start.1 = (bf16[2,8,64,128]{3,2,1,0:T(8,128)(2,1)S(1)}, bf16[2,8,64,128]{3,2,1,0:T(8,128)(2,1)S(1)}, u32[]{:S(2)}, u32[]{:S(2)}) collective-permute-start(bf16[2,8,64,128]{3,2,1,0:T(8,128)(2,1)S(1)} %dynamic-slice_bitcast_fusion), channel_id=1, source_target_pairs={{0,1},{1,0},{2,3},{3,2},{4,5},{5,4},{6,7},{7,6},{8,9},{9,8},{10,11... | collective-permute-start | bytes 786440 | tf_op jit(solution)/shard_map/ppermute | solution.py:396
  22.2 31.0 %all-to-all-start = ((bf16[256,8,128]{2,1,0:T(8,128)(2,1)}), bf16[256,8,128]{2,1,0:T(8,128)(2,1)S(1)}, u32[]{:S(2)}, u32[]{:S(2)}) async-start(bf16[256,8,128]{2,1,0:T(8,128)(2,1)} %bitcast.12), calls=%async_computation | async-start | bytes 1048576 | tf_op jit(solution)/shard_map/all_to_all | solution.py:405
